TPU v7x, 256 devices: a whole 4x4x8 slice. The times are simulated.
256 devices in a mesh: gx: 16 (over y, z_lo), gy: 8 (over x, z_hi), gz: 2 (over core).
Axes of the slice: x: 4, y: 4, z: 8 (z_hi: 2, z_lo: 4; z = z_hi * 4 + z_lo), core: 2. Of those that a mesh axis runs over, the one named last changes fastest.
Arguments:
- adjoint_start: float32 [5, 125, 32768], P(None, None, ('gx', 'gy', 'gz')), may hold values from -6 to 6
- adjoint_source: float32 [5, 125, 32768], P(None, None, ('gx', 'gy', 'gz')), may hold values from -24 to 24
- density: float32 [125, 32768], P(None, ('gx', 'gy', 'gz')), may hold values from 0.5 to 2
- velocity: float32 [3, 125, 32768], P(None, None, ('gx', 'gy', 'gz')), may hold values from -2.5 to 2.5
- pressure: float32 [125, 32768], P(None, ('gx', 'gy', 'gz')), may hold values from 0.5 to 2
- pseudo_shift: float32 [32, 64, 16], P('gx', 'gy', 'gz'), may hold values from 8 to 16
- block_inverse: float32 [5, 5, 32, 64, 16], P(None, None, 'gx', 'gy', 'gz'), may hold values from -0.02 to 0.12, as said below
Outputs:
- adjoint: float32 [5, 125, 32768], P(None, None, ('gx', 'gy', 'gz'))
Inputs may be any that keep to these rules, and one draw needn't show every extreme that they name: `block_inverse`: diagonal entries lie in 0.06 to 0.12, the others within 0.02 of zero.
All inputs are finite; a program needn't handle non-finite values.
Results may differ from a plain program's by a relative error of at most 0.0001.
Values sent between devices are 32-bit elements; how exact they have to be, the bound alone decides.
A program may use at most 64 MiB of HBM per device.

v0:
```python
import itertools

import jax
import jax.numpy as jnp
import ml_dtypes
import numpy as np
from jax import lax
from jax.experimental import pallas as pl
from jax.experimental.pallas import tpu as pltpu
from jax.sharding import PartitionSpec as P

OMEGA = 0.7
METRIC = 0.25
FINE_FACE = 0.5 * 0.25 / 0.1
COARSE_FACE = 0.5 * 0.25 * 3.0
MESH = pl.DeviceIdType.MESH
AXES = ("gx", "gy", "gz")
COUNTS = (2, 8, 8)
STRIDES = (64, 8, 1)
F32 = jnp.float32
BF16 = jnp.bfloat16


def diff_table(nodes):
    count = len(nodes)
    weights = np.array(
        [1.0 / np.prod([nodes[j] - nodes[k] for k in range(count) if k != j]) for j in range(count)]
    )
    table = np.zeros((count, count))
    for i in range(count):
        for j in range(count):
            if i != j:
                table[i, j] = weights[j] / weights[i] / (nodes[i] - nodes[j])
        table[i, i] = -np.sum(table[i])
    return table.astype(np.float32).astype(np.float64)


def fine_points():
    return np.array([-1.0, -np.sqrt(3.0 / 7.0), 0.0, np.sqrt(3.0 / 7.0), 1.0])


def interp_table():
    points = fine_points()
    table = np.stack(
        [points * (points - 1.0) / 2.0, 1.0 - points**2, points * (points + 1.0) / 2.0], axis=1
    )
    return table.astype(np.float32).astype(np.float64)


def triple(a, b, c):
    return np.kron(np.kron(a, b), c)


def padded(matrix, rows, columns):
    result = np.zeros((rows, columns))
    result[: matrix.shape[0], : matrix.shape[1]] = matrix
    return result


def face_tables(count, rows, width):
    take = np.zeros((6 * rows, width))
    give = np.zeros((width, 6 * rows))
    for dim in range(3):
        for side in range(2):
            face = 2 * dim + side
            for row in range(rows):
                a, b = divmod(min(row, count * count - 1), count)
                place = [a, b]
                place.insert(dim, side * (count - 1))
                node = (place[0] * count + place[1]) * count + place[2]
                take[face * rows + row, node] = 1.0
                if row < count * count:
                    give[node, face * rows + row] = 1.0
    return take, give


def volume_table(count, width):
    table = diff_table(fine_points() if count == 5 else np.array([-1.0, 0.0, 1.0]))
    unit = np.eye(count)
    parts = []
    for dim in range(3):
        mats = [unit, unit, unit]
        mats[dim] = -METRIC * table.T
        parts.append(padded(triple(*mats), width, width))
    return np.concatenate(parts)


def two(matrix):
    high = matrix.astype(ml_dtypes.bfloat16)
    return np.concatenate([high, high], axis=1)


def three(matrix):
    high = matrix.astype(ml_dtypes.bfloat16)
    low = (matrix - high.astype(np.float64)).astype(ml_dtypes.bfloat16)
    return np.concatenate([high, high, low], axis=1)


def tables():
    prolong = interp_table()
    take, give = face_tables(5, 32, 128)
    take_c, give_c = face_tables(3, 16, 32)
    pick = np.zeros((32, 128))
    for n, (a, b, c) in enumerate(itertools.product(range(3), repeat=3)):
        pick[n, (2 * a * 5 + 2 * b) * 5 + 2 * c] = 1.0
    restrict = padded(triple(prolong.T, prolong.T, prolong.T), 32, 128)
    restrict = np.concatenate([restrict, take_c @ restrict])
    extend = padded(triple(prolong, prolong, prolong), 128, 32)
    flat = np.kron(prolong, prolong)
    flat = np.concatenate([flat, np.repeat(flat[24:25], 7, axis=0)])
    face_extend = np.zeros((192, 96))
    for face in range(6):
        face_extend[32 * face : 32 * face + 32, 16 * face : 16 * face + 9] = flat
    return {
        "take": two(np.concatenate([take, pick, take_c @ pick])),
        "volume": three(volume_table(5, 128)),
        "give": two(-FINE_FACE * np.concatenate([take @ give, give])),
        "restrict": three(restrict),
        "restrict_give": three(-FINE_FACE * restrict @ give),
        "volume_c": two(np.concatenate([volume_table(3, 32), take_c])),
        "give_c": two(-COARSE_FACE * np.concatenate([take_c @ give_c, give_c])),
        "extend": three(extend),
        "face_extend": three(face_extend),
    }


def dot(matrix, field):
    return jnp.dot(matrix, field, preferred_element_type=F32)


def split(value):
    high = value.astype(BF16)
    low = (value - high.astype(F32)).astype(BF16)
    return high, low


def lanes(var):
    return slice(128 * var, 128 * var + 128)


def rows_of(step, size=16):
    return pl.ds(pl.multiple_of(step * size, size), size)


def load(ref, rows):
    return [ref[rows, lanes(v)] for v in range(5)]


def store(ref, rows, values):
    for v in range(5):
        ref[rows, lanes(v)] = values[v]


def store_split(ref, step, height, values, pieces):
    for v in range(5):
        parts = split(values[v])
        for piece in range(pieces):
            ref[rows_of(step + piece * (height // 16)), lanes(v)] = parts[piece % 2]


def pull_all(cot, state):
    w = state[:3]
    enthalpy = state[3]
    crossed = [w[0] * c[1] + w[1] * c[2] + w[2] * c[3] + enthalpy * c[4] for c in cot]
    ends = [w[d] * cot[d][4] for d in range(3)]
    energy = ends[0] + ends[1] + ends[2]
    total = 0.4 * (cot[0][1] + cot[1][2] + cot[2][3] + energy)
    half_square = 0.5 * (w[0] * w[0] + w[1] * w[1] + w[2] * w[2])
    first = half_square * total - (w[0] * crossed[0] + w[1] * crossed[1] + w[2] * crossed[2])
    middle = []
    for j in range(3):
        drift = w[0] * cot[0][1 + j] + w[1] * cot[1][1 + j] + w[2] * cot[2][1 + j]
        middle.append(drift + cot[j][0] + crossed[j] - w[j] * total)
    return [first, *middle, total + energy]


def pull_face(jump, state, speed, normal, pick, sign):
    w = state[:3]
    crossed = w[0] * jump[1] + w[1] * jump[2] + w[2] * jump[3] + state[3] * jump[4]
    end = speed * jump[4]
    total = 0.4 * (normal + end)
    half_square = 0.5 * (w[0] * w[0] + w[1] * w[1] + w[2] * w[2])
    turned = jump[0] + crossed
    out = [half_square * total - speed * crossed]
    for j in range(3):
        out.append(speed * jump[1 + j] - w[j] * total + pick[j] * turned)
    out.append(total + end)
    top = jnp.abs(speed) + state[4]
    return [sign * out[v] + top * jump[v] for v in range(5)]


def apply_blocks(blocks, values):
    result = []
    for a in range(5):
        total = blocks[a] * values[0]
        for b in range(1, 5):
            total = total + blocks[b * 5 + a] * values[b]
        result.append(total)
    return result


def kernel(start_h, source_h, density_h, velocity_h, pressure_h, shift_h, inverse_h, *rest):
    tables_h, rest = rest[:9], rest[9:]
    out_h, rest = rest[0], rest[1:]
    (start_r, source_r, density_r, velocity_r, pressure_r, shift_r, inverse_r), rest = rest[:7], rest[7:]
    tables_r, rest = rest[:9], rest[9:]
    (take, volume, give, restrict, restrict_give, volume_c, give_c, extend, face_extend) = tables_r
    (
        field, source, state, base, split_n, cot,
        face_state, face_field, jump, split_f, compact, own,
        state_c, field_c, base_c, split_c, split_cf, cot_c, jump_c, compact_c, own_c,
        blocks, shift, out_r,
    ), rest = rest[:24], rest[24:]
    send_fine, recv_fine, send_coarse, recv_coarse, rest = rest[:6], rest[6:12], rest[12:18], rest[18:24], rest[24:]
    in_sems, out_sem, send_sems, recv_sems = rest

    place = [lax.axis_index(axis) for axis in AXES]
    size = [lax.axis_size(axis) for axis in AXES]
    has = [place[f // 2] > 0 if f % 2 == 0 else place[f // 2] < size[f // 2] - 1 for f in range(6)]

    def partner(f):
        target = list(place)
        target[f // 2] = target[f // 2] + (1 if f % 2 else -1)
        return tuple(target)

    barrier = pltpu.get_barrier_semaphore()
    for f in range(6):
        @pl.when(has[f])
        def _(f=f):
            pl.semaphore_signal(barrier, inc=1, device_id=partner(f), device_id_type=MESH)

    field[120:128, :] = jnp.zeros((8, 640), F32)
    source[120:128, :] = jnp.zeros((8, 640), F32)
    order = [
        (start_h, start_r), (tables_h[0], take), (velocity_h, velocity_r), (density_h, density_r),
        (pressure_h, pressure_r), (tables_h[1], volume), (source_h, source_r), (shift_h, shift_r),
        (inverse_h, inverse_r), (tables_h[2], give),
    ] + [(tables_h[n], tables_r[n]) for n in range(3, 9)]
    inward = [pltpu.make_async_copy(a, b, in_sems.at[n]) for n, (a, b) in enumerate(order)]
    for copy in inward:
        copy.start()

    def lane_place(rows, dim):
        lane = lax.broadcasted_iota(jnp.int32, (rows, 128), 1)
        return (lane // STRIDES[dim]) % COUNTS[dim]

    def gather_faces(source_ref, offset, rows, whole, target):
        sub = lax.broadcasted_iota(jnp.int32, (8, 128), 0)

        def one(f, _):
            top = offset + f * rows
            last = source_ref[pl.ds(pl.multiple_of(top + whole, 8), 8), lanes(0)]
            for v in range(5):
                target[f, whole * v : whole * v + whole, :] = source_ref[
                    pl.ds(pl.multiple_of(top, 8), whole), lanes(v)
                ]
                if v:
                    here = source_ref[pl.ds(pl.multiple_of(top + whole, 8), 8), lanes(v)]
                    last = jnp.where(sub == v, here, last)
            target[f, 5 * whole : 5 * whole + 8, :] = last
            return 0

        lax.fori_loop(0, 6, one, 0)

    def scatter_faces(source_ref, rows, whole, target):
        def one(f, _):
            top = f * rows
            for v in range(5):
                target[pl.ds(pl.multiple_of(top, 8), whole), lanes(v)] = source_ref[
                    f, whole * v : whole * v + whole, :
                ]
                target[pl.ds(pl.multiple_of(top + whole, 8), 8), lanes(v)] = jnp.broadcast_to(
                    source_ref[f, pl.ds(5 * whole + v, 1), :], (8, 128)
                )
            return 0

        lax.fori_loop(0, 6, one, 0)

    def turn(value, amount):
        amount %= 128
        return pltpu.roll(value, amount, 1) if amount else value

    def copies(exchange, sends, receives):
        row = exchange + (2 if sends is send_coarse else 0)
        return [
            pltpu.make_async_remote_copy(
                src_ref=sends[f].at[exchange],
                dst_ref=receives[f ^ 1].at[exchange],
                send_sem=send_sems.at[row, f],
                recv_sem=recv_sems.at[row, f ^ 1],
                device_id=partner(f),
                device_id_type=MESH,
            )
            for f in range(6)
        ]

    def send(exchange, faces, sends, remote):
        for f in range(6):
            dim, side = divmod(f, 2)
            count, stride = COUNTS[dim], STRIDES[dim]
            slot = sends[f].shape[1]
            where = lane_place(slot, dim)
            packed = None
            for g in range(faces.shape[1] // slot):
                block = turn(faces[f, g * slot : g * slot + slot, :], (g - side * (count - 1)) * stride)
                packed = block if packed is None else jnp.where(where == g, block, packed)
            sends[f][exchange] = packed
            if exchange == 0 and sends is send_fine and f == 0:
                pl.semaphore_wait(barrier, sum(h.astype(jnp.int32) for h in has))

            @pl.when(has[f])
            def _():
                remote[f].start()

    def own_part(faces, result):
        for f in range(6):
            dim, side = divmod(f, 2)
            count, stride = COUNTS[dim], STRIDES[dim]
            inside = lane_place(faces.shape[1], dim) != side * (count - 1)
            other = turn(faces[f ^ 1], -stride if side else stride)
            result[f] = faces[f] - jnp.where(inside, other, 0.0)

    def receive(exchange, receives, remote, result, target):
        for f in range(6):
            dim, side = divmod(f, 2)
            count, stride = COUNTS[dim], STRIDES[dim]
            slot = receives[f].shape[1]
            edge = lane_place(slot, dim) == side * (count - 1)

            @pl.when(has[f])
            def _():
                remote[f ^ 1].wait_recv()
                packed = receives[f][exchange]
                for g in range(result.shape[1] // slot):
                    here = slice(g * slot, g * slot + slot)
                    there = turn(packed, (side * (count - 1) - g) * stride)
                    target[f, here, :] = result[f, here, :] - jnp.where(edge, there, 0.0)

            @pl.when(jnp.logical_not(has[f]))
            def _():
                target[f] = result[f]

    def face_pull(step, values, state_ref, offset, per_face):
        f = lax.div(step, per_face)
        d = lax.div(f, 2)
        sign = (2 * (f - 2 * d) - 1).astype(F32)
        pick = [(d == j).astype(F32) for j in range(3)]
        rows = rows_of(step + offset)
        local = load(state_ref, rows)
        speed = state_ref[rows, pl.ds(pl.multiple_of(d * 128, 128), 128)]
        normal = pick[0] * values[1] + pick[1] * values[2] + pick[2] * values[3]
        return pull_face(values, local, speed, normal, pick, sign)

    def block_rows():
        return [blocks[n] for n in range(25)]

    inward[0].wait()
    for v in range(5):
        field[0:125, lanes(v)] = start_r[v]

    def split_field(step, _):
        store_split(split_n, step, 128, load(field, rows_of(step)), 3)
        return 0

    lax.fori_loop(0, 8, split_field, 0)
    inward[1].wait()
    face_field[...] = dot(take[0:192, :], split_n[0:256, :])
    gather_faces(face_field, 0, 32, 24, compact)
    fine_0 = copies(0, send_fine, recv_fine)
    send(0, compact, send_fine, fine_0)

    for n in (2, 3, 4):
        inward[n].wait()
    state[120:128, :] = jnp.zeros((8, 640), F32)
    for part in ((0, 64), (64, 125)):
        here = slice(*part)
        w = [velocity_r[d, here, :] for d in range(3)]
        sound_2 = 1.4 * pressure_r[here, :] / density_r[here, :]
        for d in range(3):
            state[here, lanes(d)] = w[d]
        state[here, lanes(3)] = 2.5 * sound_2 + 0.5 * (w[0] * w[0] + w[1] * w[1] + w[2] * w[2])
        state[here, lanes(4)] = jnp.sqrt(sound_2)

    def split_state(step, _):
        store_split(split_f, step, 128, load(state, rows_of(step)), 2)
        return 0

    lax.fori_loop(0, 8, split_state, 0)
    face_state[...] = dot(take[0:192, :], split_f[0:256, :])
    state_c[...] = dot(take[192:320, :], split_f[0:256, :])
    own_part(compact, own)

    for n in (7, 8):
        inward[n].wait()
    spread = (
        lax.broadcasted_iota(jnp.int32, (8, 128), 1) % 8 == lax.broadcasted_iota(jnp.int32, (8, 128), 0)
    ).astype(F32)

    def to_lanes(value, count):
        wide = jnp.dot(
            value.reshape(16 * count, 8), spread,
            precision=lax.Precision.HIGHEST, preferred_element_type=F32,
        ).reshape(count, 16, 128)
        row = lax.broadcasted_iota(jnp.int32, (count, 16, 128), 1)
        lane = lax.broadcasted_iota(jnp.int32, (count, 16, 128), 2)
        kept = jnp.where(lane // 8 == row, wide, 0.0)
        return jnp.broadcast_to(jnp.sum(kept, axis=1, keepdims=True), (count, 16, 128))

    shift[...] = to_lanes(shift_r[...], 1)[0]
    blocks[...] = OMEGA * to_lanes(inverse_r[...], 25)

    inward[5].wait()
    inward[6].wait()
    for v in range(5):
        source[0:125, lanes(v)] = source_r[v]

    def residual(step, height, cot_ref, values, right, state_ref):
        rows = rows_of(step)
        cots = [load(cot_ref, rows_of(step + d * (height // 16))) for d in range(3)]
        pulled = pull_all(cots, load(state_ref, rows))
        return [right[v] - shift[...] * values[v] - pulled[v] for v in range(5)]

    def smooth_volume(step, _, keep_split):
        rows = rows_of(step)
        values = load(field, rows)
        resid = residual(step, 128, cot, values, load(source, rows), state)
        change = apply_blocks(block_rows(), resid)
        values = [values[v] + change[v] for v in range(5)]
        store(base, rows, values)
        if keep_split:
            store_split(split_n, step, 128, values, 2)
        return 0

    cot[...] = dot(volume[...], split_n[...])
    lax.fori_loop(0, 8, lambda s, c: smooth_volume(s, c, True), 0)
    face_field[...] = dot(take[0:192, :], split_n[0:256, :])

    def smooth_faces(step, _):
        values = face_pull(step, load(jump, rows_of(step)), face_state, 0, 2)
        store_split(split_f, step, 192, apply_blocks(block_rows(), values), 2)
        return 0

    receive(0, recv_fine, fine_0, own, compact)
    scatter_faces(compact, 32, 24, jump)
    lax.fori_loop(0, 12, smooth_faces, 0)
    inward[9].wait()
    face_field[...] += dot(give[0:192, :], split_f[0:384, :])
    gather_faces(face_field, 0, 32, 24, compact)
    fine_1 = copies(1, send_fine, recv_fine)
    send(1, compact, send_fine, fine_1)

    for n in range(10, 16):
        inward[n].wait()
    field[...] = base[...] + dot(give[192:320, :], split_f[0:384, :])
    own_part(compact, own)
    lax.fori_loop(0, 8, split_field, 0)
    cot[...] = dot(volume[...], split_n[...])

    def residual_volume(step, _):
        rows = rows_of(step)
        resid = residual(step, 128, cot, load(field, rows), load(source, rows), state)
        store_split(split_n, step, 128, resid, 3)
        return 0

    lax.fori_loop(0, 8, residual_volume, 0)
    field_c[...] = dot(restrict[...], split_n[...])

    def residual_faces(step, _):
        values = face_pull(step, load(jump, rows_of(step)), face_state, 0, 2)
        store_split(split_f, step, 192, values, 3)
        return 0

    receive(1, recv_fine, fine_1, own, compact)
    scatter_faces(compact, 32, 24, jump)
    lax.fori_loop(0, 12, residual_faces, 0)
    field_c[...] += dot(restrict_give[...], split_f[...])

    def coarse_first(step, _):
        rows = rows_of(step)
        store(base_c, rows, apply_blocks(block_rows(), load(field_c, rows)))
        return 0

    lax.fori_loop(0, 8, coarse_first, 0)
    gather_faces(base_c, 32, 16, 8, compact_c)
    coarse_0 = copies(0, send_coarse, recv_coarse)
    send(0, compact_c, send_coarse, coarse_0)
    own_part(compact_c, own_c)

    def split_coarse(step, _):
        store_split(split_c, step, 32, load(base_c, rows_of(step)), 2)
        return 0

    lax.fori_loop(0, 2, split_coarse, 0)
    cot_c[...] = dot(volume_c[0:96, :], split_c[0:64, :])

    def coarse_volume(step, _):
        rows = rows_of(step)
        values = load(base_c, rows)
        resid = residual(step, 32, cot_c, values, load(field_c, rows), state_c)
        change = apply_blocks(block_rows(), resid)
        values = [values[v] + change[v] for v in range(5)]
        store(field_c, rows, values)
        store_split(split_c, step, 32, values, 2)
        return 0

    lax.fori_loop(0, 2, coarse_volume, 0)
    base_c[32:128, :] = dot(volume_c[96:192, :], split_c[0:64, :])

    def coarse_faces(step, _):
        values = face_pull(step, load(jump_c, rows_of(step)), state_c, 2, 1)
        store_split(split_cf, step, 96, apply_blocks(block_rows(), values), 2)
        return 0

    receive(0, recv_coarse, coarse_0, own_c, compact_c)
    scatter_faces(compact_c, 16, 8, jump_c)
    lax.fori_loop(0, 6, coarse_faces, 0)
    base_c[32:128, :] += dot(give_c[0:96, :], split_cf[0:192, :])
    gather_faces(base_c, 32, 16, 8, compact_c)
    coarse_1 = copies(1, send_coarse, recv_coarse)
    send(1, compact_c, send_coarse, coarse_1)

    base_c[0:32, :] = field_c[0:32, :] + dot(give_c[96:128, :], split_cf[0:192, :])
    own_part(compact_c, own_c)

    def split_coarse_3(step, _):
        store_split(split_c, step, 32, load(base_c, rows_of(step)), 3)
        return 0

    lax.fori_loop(0, 2, split_coarse_3, 0)
    field[...] += dot(extend[...], split_c[...])
    lax.fori_loop(0, 8, split_field, 0)
    cot[...] = dot(volume[...], split_n[...])
    lax.fori_loop(0, 8, lambda s, c: smooth_volume(s, c, False), 0)

    def split_jump(step, _):
        store_split(split_cf, step, 96, load(jump_c, rows_of(step)), 3)
        return 0

    receive(1, recv_coarse, coarse_1, own_c, compact_c)
    scatter_faces(compact_c, 16, 8, jump_c)
    lax.fori_loop(0, 6, split_jump, 0)
    jump[...] += dot(face_extend[...], split_cf[...])
    lax.fori_loop(0, 12, smooth_faces, 0)
    base[...] += dot(give[192:320, :], split_f[0:384, :])
    for v in range(5):
        out_r[v] = base[0:125, lanes(v)]
    outward = pltpu.make_async_copy(out_r, out_h, out_sem)
    outward.start()
    for n, remote in enumerate((fine_0, fine_1, coarse_0, coarse_1)):
        for f in range(6):
            @pl.when(has[f])
            def _(remote=remote, f=f):
                remote[f].wait_send()
    outward.wait()


def body(*args):
    constants = [jnp.asarray(table) for table in tables().values()]
    vmem = pltpu.VMEM
    raw = [vmem(a.shape, a.dtype) for a in args]
    held = [vmem(t.shape, t.dtype) for t in constants]
    work = [
        vmem((128, 640), F32), vmem((128, 640), F32), vmem((128, 640), F32), vmem((128, 640), F32),
        vmem((384, 640), BF16), vmem((384, 640), F32),
        vmem((192, 640), F32), vmem((192, 640), F32), vmem((192, 640), F32), vmem((576, 640), BF16),
        vmem((6, 128, 128), F32), vmem((6, 128, 128), F32),
        vmem((128, 640), F32), vmem((128, 640), F32), vmem((128, 640), F32), vmem((96, 640), BF16),
        vmem((288, 640), BF16), vmem((96, 640), F32), vmem((96, 640), F32),
        vmem((6, 48, 128), F32), vmem((6, 48, 128), F32),
        vmem((25, 16, 128), F32), vmem((16, 128), F32), vmem(args[0].shape, F32),
    ]
    fine = [vmem((2, rows, 128), F32) for rows in (64, 64, 16, 16, 16, 16)]
    coarse = [vmem((2, rows, 128), F32) for rows in (24, 24, 8, 8, 8, 8)]
    sems = [
        pltpu.SemaphoreType.DMA((16,)),
        pltpu.SemaphoreType.DMA,
        pltpu.SemaphoreType.DMA((4, 6)),
        pltpu.SemaphoreType.DMA((4, 6)),
    ]
    anywhere = pl.BlockSpec(memory_space=pl.ANY)
    return pl.pallas_call(
        kernel,
        out_shape=jax.ShapeDtypeStruct(args[0].shape, F32),
        in_specs=[anywhere] * (len(args) + len(constants)),
        out_specs=anywhere,
        scratch_shapes=raw + held + work + fine + fine + coarse + coarse + sems,
        compiler_params=pltpu.CompilerParams(
            collective_id=0, has_side_effects=True, vmem_limit_bytes=40 * 1024 * 1024
        ),
    )(*args, *constants)


def solution(mesh):
    in_specs = (
        P(None, None, AXES),
        P(None, None, AXES),
        P(None, AXES),
        P(None, None, AXES),
        P(None, AXES),
        P(*AXES),
        P(None, None, *AXES),
    )
    return jax.shard_map(
        body, mesh=mesh, in_specs=in_specs, out_specs=P(None, None, AXES), check_vma=False
    )
```

profile of v0, /device:TPU:30, one launch (start us, length us, event | category | flops | bytes accessed | tf_op | source)
XLA Modules:
  0.0 50.2 jit_solution(241077118532462549)
XLA Ops:
  0.0 0.0 copy-start
  0.0 1.0 %copy-done = f32[5,125,128]{2,1,0:T(8,128)S(1)} copy-done((f32[5,125,128]{2,1,0:T(8,128)S(1)}, f32[5,125,128]{2,1,0:T(8,128)}, u32[]{:S(2)}) %copy-start) | copy-done | bytes 320024
  1.0 0.0 copy-start.1
  1.0 1.0 %copy-done.1 = f32[5,125,128]{2,1,0:T(8,128)S(1)} copy-done((f32[5,125,128]{2,1,0:T(8,128)S(1)}, f32[5,125,128]{2,1,0:T(8,128)}, u32[]{:S(2)}) %copy-start.1) | copy-done | bytes 320024
  1.9 0.0 copy-start.2
  1.9 1.0 %copy-done.2 = bf16[384,384]{1,0:T(8,128)(2,1)S(1)} copy-done((bf16[384,384]{1,0:T(8,128)(2,1)S(1)}, bf16[384,384]{1,0:T(8,128)(2,1)}, u32[]{:S(2)}) %copy-start.2) | copy-done | bytes 294936
  2.9 0.0 copy-start.3
  2.9 0.9 %copy-done.3 = bf16[320,384]{1,0:T(8,128)(2,1)S(1)} copy-done((bf16[320,384]{1,0:T(8,128)(2,1)S(1)}, bf16[320,384]{1,0:T(8,128)(2,1)}, u32[]{:S(2)}) %copy-start.3) | copy-done | bytes 245784
  3.9 0.0 copy-start.4
  3.9 0.9 %copy-done.4 = f32[5,5,2,8,8]{4,3,2,1,0:T(8,128)S(1)} copy-done((f32[5,5,2,8,8]{4,3,2,1,0:T(8,128)S(1)}, f32[5,5,2,8,8]{4,3,2,1,0:T(8,128)}, u32[]{:S(2)}) %copy-start.4) | copy-done | bytes 12824
  4.8 0.0 copy-start.5
  4.8 0.9 %copy-done.5 = f32[3,125,128]{2,1,0:T(8,128)S(1)} copy-done((f32[3,125,128]{2,1,0:T(8,128)S(1)}, f32[3,125,128]{2,1,0:T(8,128)}, u32[]{:S(2)}) %copy-start.5) | copy-done | bytes 192024
  5.7 0.0 copy-start.6
  5.7 0.9 %copy-done.6 = bf16[128,576]{1,0:T(8,128)(2,1)S(1)} copy-done((bf16[128,576]{1,0:T(8,128)(2,1)S(1)}, bf16[128,576]{1,0:T(8,128)(2,1)}, u32[]{:S(2)}) %copy-start.6) | copy-done | bytes 147480
  6.6 0.0 copy-start.7
  6.6 0.9 %copy-done.7 = bf16[320,256]{1,0:T(8,128)(2,1)S(1)} copy-done((bf16[320,256]{1,0:T(8,128)(2,1)S(1)}, bf16[320,256]{1,0:T(8,128)(2,1)}, u32[]{:S(2)}) %copy-start.7) | copy-done | bytes 163864
  7.5 0.0 copy-start.8
  7.5 0.9 %copy-done.8 = bf16[192,288]{1,0:T(8,128)(2,1)S(1)} copy-done((bf16[192,288]{1,0:T(8,128)(2,1)S(1)}, bf16[192,288]{1,0:T(8,128)(2,1)}, u32[]{:S(2)}) %copy-start.8) | copy-done | bytes 110616
  8.5 0.0 copy-start.9
  8.5 0.9 %copy-done.9 = bf16[128,384]{1,0:T(8,128)(2,1)S(1)} copy-done((bf16[128,384]{1,0:T(8,128)(2,1)S(1)}, bf16[128,384]{1,0:T(8,128)(2,1)}, u32[]{:S(2)}) %copy-start.9) | copy-done | bytes 98328
  9.3 0.0 copy-start.10
  9.3 0.8 %copy-done.10 = f32[125,128]{1,0:T(8,128)S(1)} copy-done((f32[125,128]{1,0:T(8,128)S(1)}, f32[125,128]{1,0:T(8,128)}, u32[]{:S(2)}) %copy-start.10) | copy-done | bytes 64024
  10.2 0.0 copy-start.11
  10.2 0.8 %copy-done.11 = f32[125,128]{1,0:T(8,128)S(1)} copy-done((f32[125,128]{1,0:T(8,128)S(1)}, f32[125,128]{1,0:T(8,128)}, u32[]{:S(2)}) %copy-start.11) | copy-done | bytes 64024
  11.0 0.0 copy-start.12
  11.0 0.8 %copy-done.12 = bf16[128,192]{1,0:T(8,128)(2,1)S(1)} copy-done((bf16[128,192]{1,0:T(8,128)(2,1)S(1)}, bf16[128,192]{1,0:T(8,128)(2,1)}, u32[]{:S(2)}) %copy-start.12) | copy-done | bytes 49176
  11.9 0.0 copy-start.13
  11.9 0.8 %copy-done.13 = bf16[192,64]{1,0:T(8,128)(2,1)S(1)} copy-done((bf16[192,64]{1,0:T(8,128)(2,1)S(1)}, bf16[192,64]{1,0:T(8,128)(2,1)}, u32[]{:S(2)}) %copy-start.13) | copy-done | bytes 24600
  12.7 0.0 copy-start.14
  12.7 0.8 %copy-done.14 = bf16[128,96]{1,0:T(8,128)(2,1)S(1)} copy-done((bf16[128,96]{1,0:T(8,128)(2,1)S(1)}, bf16[128,96]{1,0:T(8,128)(2,1)}, u32[]{:S(2)}) %copy-start.14) | copy-done | bytes 24600
  13.4 0.0 copy-start.15
  13.4 0.7 %copy-done.15 = f32[2,8,8]{2,1,0:T(8,128)S(1)} copy-done((f32[2,8,8]{2,1,0:T(8,128)S(1)}, f32[2,8,8]{2,1,0:T(8,128)}, u32[]{:S(2)}) %copy-start.15) | copy-done | bytes 536
  14.1 35.3 %shard_map.154 = f32[5,125,128]{2,1,0:T(8,128)S(1)} custom-call(f32[5,125,128]{2,1,0:T(8,128)S(1)} %copy-done, f32[5,125,128]{2,1,0:T(8,128)S(1)} %copy-done.1, f32[125,128]{1,0:T(8,128)S(1)} %copy-done.10, f32[3,125,128]{2,1,0:T(8,128)S(1)} %copy-done.5, f32[125,128]{1,0:T(8,128)S(1)} %copy-done.11, f32[2,8,8]{2,1,0:T(8,128)S(1)} %copy-done.15, ...), custom_call_target="tpu_custom_call" | custom-call | tf_op jit(solution)/shard_map/pallas_call | solution.py:581
  49.4 0.7 %copy.18 = f32[5,125,128]{2,1,0:T(8,128)} copy(f32[5,125,128]{2,1,0:T(8,128)S(1)} %shard_map.154) | data formatting | bytes 640000
Async XLA Ops:
  0.0 1.0 %copy-start = (f32[5,125,128]{2,1,0:T(8,128)S(1)}, f32[5,125,128]{2,1,0:T(8,128)}, u32[]{:S(2)}) copy-start(f32[5,125,128]{2,1,0:T(8,128)} %start_h.1) | copy-start | bytes 960004
  1.0 1.0 %copy-start.1 = (f32[5,125,128]{2,1,0:T(8,128)S(1)}, f32[5,125,128]{2,1,0:T(8,128)}, u32[]{:S(2)}) copy-start(f32[5,125,128]{2,1,0:T(8,128)} %source_h.1) | copy-start | bytes 960004
  1.9 1.0 %copy-start.2 = (bf16[384,384]{1,0:T(8,128)(2,1)S(1)}, bf16[384,384]{1,0:T(8,128)(2,1)}, u32[]{:S(2)}) copy-start(bf16[384,384]{1,0:T(8,128)(2,1)} %constant.19.clone.rest_1_) | copy-start | bytes 884740
  2.9 0.9 %copy-start.3 = (bf16[320,384]{1,0:T(8,128)(2,1)S(1)}, bf16[320,384]{1,0:T(8,128)(2,1)}, u32[]{:S(2)}) copy-start(bf16[320,384]{1,0:T(8,128)(2,1)} %constant.20.clone.rest_2_) | copy-start | bytes 737284
  3.9 0.9 %copy-start.4 = (f32[5,5,2,8,8]{4,3,2,1,0:T(8,128)S(1)}, f32[5,5,2,8,8]{4,3,2,1,0:T(8,128)}, u32[]{:S(2)}) copy-start(f32[5,5,2,8,8]{4,3,2,1,0:T(8,128)} %inverse_h.1) | copy-start | bytes 38404
  4.8 0.9 %copy-start.5 = (f32[3,125,128]{2,1,0:T(8,128)S(1)}, f32[3,125,128]{2,1,0:T(8,128)}, u32[]{:S(2)}) copy-start(f32[3,125,128]{2,1,0:T(8,128)} %velocity_h.1) | copy-start | bytes 576004
  5.7 0.9 %copy-start.6 = (bf16[128,576]{1,0:T(8,128)(2,1)S(1)}, bf16[128,576]{1,0:T(8,128)(2,1)}, u32[]{:S(2)}) copy-start(bf16[128,576]{1,0:T(8,128)(2,1)} %constant.22.clone.rest_4_) | copy-start | bytes 442372
  6.6 0.9 %copy-start.7 = (bf16[320,256]{1,0:T(8,128)(2,1)S(1)}, bf16[320,256]{1,0:T(8,128)(2,1)}, u32[]{:S(2)}) copy-start(bf16[320,256]{1,0:T(8,128)(2,1)} %constant.18.clone.rest_0_) | copy-start | bytes 491524
  7.5 0.9 %copy-start.8 = (bf16[192,288]{1,0:T(8,128)(2,1)S(1)}, bf16[192,288]{1,0:T(8,128)(2,1)}, u32[]{:S(2)}) copy-start(bf16[192,288]{1,0:T(8,128)(2,1)} %constant.26.clone.rest_8_) | copy-start | bytes 331780
  8.5 0.9 %copy-start.9 = (bf16[128,384]{1,0:T(8,128)(2,1)S(1)}, bf16[128,384]{1,0:T(8,128)(2,1)}, u32[]{:S(2)}) copy-start(bf16[128,384]{1,0:T(8,128)(2,1)} %constant.21.clone.rest_3_) | copy-start | bytes 294916
  9.3 0.8 %copy-start.10 = (f32[125,128]{1,0:T(8,128)S(1)}, f32[125,128]{1,0:T(8,128)}, u32[]{:S(2)}) copy-start(f32[125,128]{1,0:T(8,128)} %density_h.1) | copy-start | bytes 192004
  10.2 0.8 %copy-start.11 = (f32[125,128]{1,0:T(8,128)S(1)}, f32[125,128]{1,0:T(8,128)}, u32[]{:S(2)}) copy-start(f32[125,128]{1,0:T(8,128)} %pressure_h.1) | copy-start | bytes 192004
  11.0 0.8 %copy-start.12 = (bf16[128,192]{1,0:T(8,128)(2,1)S(1)}, bf16[128,192]{1,0:T(8,128)(2,1)}, u32[]{:S(2)}) copy-start(bf16[128,192]{1,0:T(8,128)(2,1)} %constant.24.clone.rest_6_) | copy-start | bytes 147460
  11.9 0.8 %copy-start.13 = (bf16[192,64]{1,0:T(8,128)(2,1)S(1)}, bf16[192,64]{1,0:T(8,128)(2,1)}, u32[]{:S(2)}) copy-start(bf16[192,64]{1,0:T(8,128)(2,1)} %constant.23.clone.rest_5_) | copy-start | bytes 73732
  12.7 0.8 %copy-start.14 = (bf16[128,96]{1,0:T(8,128)(2,1)S(1)}, bf16[128,96]{1,0:T(8,128)(2,1)}, u32[]{:S(2)}) copy-start(bf16[128,96]{1,0:T(8,128)(2,1)} %constant.25.clone.rest_7_) | copy-start | bytes 73732
  13.4 0.7 %copy-start.15 = (f32[2,8,8]{2,1,0:T(8,128)S(1)}, f32[2,8,8]{2,1,0:T(8,128)}, u32[]{:S(2)}) copy-start(f32[2,8,8]{2,1,0:T(8,128)} %shift_h.1) | copy-start | bytes 1540
where the time goes:
time: 50.8 us; the launch traced here: 50.2 us
  Pallas kernels  35.3 us (69%)
  local copies, waits for them, and re-layouts  14.8 us (29%)
    pallas_call x1, Pallas kernels, body(): pl.pallas_call(kernel, out_shape=jax.ShapeDtypeStruct(args[0].shape, F32)...  35.3 us
    unnamed x33, local copies, waits for them, and re-layouts  14.8 us

commit v1 on v0

--- a/solution.py
+++ b/solution.py
@@ -585,7 +585,7 @@
         out_specs=anywhere,
         scratch_shapes=raw + held + work + fine + fine + coarse + coarse + sems,
         compiler_params=pltpu.CompilerParams(
-            collective_id=0, has_side_effects=True, vmem_limit_bytes=40 * 1024 * 1024
+            collective_id=0, has_side_effects=True, vmem_limit_bytes=60 * 1024 * 1024
         ),
     )(*args, *constants)
 

time: 50.8 us -> 37.9 us (0.75); the launches traced: 50.2 us -> 37.8 us
  local copies, waits for them, and re-layouts: 14.8 us -> 1.72 us
  Pallas kernels: 35.3 us -> 36.1 us
    unnamed x33 -> x1, local copies, waits for them, and re-layouts: 14.8 us -> 1.72 us
    pallas_call x1, Pallas kernels: 35.3 us -> 36.1 us  [body(): pl.pallas_call(kernel, out_shape=jax.ShapeDtypeStruct(args[0].shape, F32)...]
where the time goes in v1:
time: 37.9 us; the launch traced here: 37.8 us
  Pallas kernels  36.1 us (95%)
  local copies, waits for them, and re-layouts  1.72 us (5%)
    pallas_call x1, Pallas kernels, body(): pl.pallas_call(kernel, out_shape=jax.ShapeDtypeStruct(args[0].shape, F32)...  36.1 us
    unnamed x1, local copies, waits for them, and re-layouts  1.72 us

profile of v1, /device:TPU:30, one launch (start us, length us, event | category | flops | bytes accessed | tf_op | source)
XLA Modules:
  0.0 37.8 jit_solution(1117563226854311873)
XLA Ops:
  0.0 36.1 %shard_map.154 = f32[5,125,128]{2,1,0:T(8,128)} custom-call(f32[5,125,128]{2,1,0:T(8,128)} %start_h.1, f32[5,125,128]{2,1,0:T(8,128)} %source_h.1, f32[125,128]{1,0:T(8,128)} %density_h.1, f32[3,125,128]{2,1,0:T(8,128)} %velocity_h.1, f32[125,128]{1,0:T(8,128)} %pressure_h.1, f32[2,8,8]{2,1,0:T(8,128)} %shift_h.1, f32[5,5,2,8,8]{4,3,2,1,0:T(8,128)} %inverse_h.1, ...), custom_call_target="tpu_custom_call" | custom-call | tf_op jit(solution)/shard_map/pallas_call | solution.py:581
  36.1 1.7 %copy.18 = f32[5,125,128]{2,1,0:T(8,128)} copy(f32[5,125,128]{2,1,0:T(8,128)} %shard_map.154) | data formatting | bytes 640000

commit v2 on v1

--- a/solution.py
+++ b/solution.py
@@ -17,6 +17,7 @@
 AXES = ("gx", "gy", "gz")
 COUNTS = (2, 8, 8)
 STRIDES = (64, 8, 1)
+LINES = [(i, j, s, t) for i, j in ((0, 1), (0, 2), (1, 2)) for s in range(2) for t in range(2)]
 F32 = jnp.float32
 BF16 = jnp.bfloat16
 
@@ -74,6 +75,32 @@
     return take, give
 
 
+def line_table(count, width):
+    take = np.zeros((96, width))
+    for line, (i, j, s, t) in enumerate(LINES):
+        for node in range(count):
+            place = [node] * 3
+            place[i], place[j] = s * (count - 1), t * (count - 1)
+            take[8 * line + node, (place[0] * count + place[1]) * count + place[2]] = 1.0
+    return take
+
+
+def line_faces(count, rows):
+    result = np.zeros((2, 6 * rows, 96))
+    for dim in range(3):
+        for side in range(2):
+            for row in range(rows):
+                pair = divmod(min(row, count * count - 1), count)
+                others = [d for d in range(3) if d != dim]
+                for n in range(2):
+                    if pair[n] % (count - 1) == 0:
+                        sides = {dim: side, others[n]: pair[n] // (count - 1)}
+                        i, j = sorted(sides)
+                        line = LINES.index((i, j, sides[i], sides[j]))
+                        result[n, (2 * dim + side) * rows + row, 8 * line + pair[1 - n]] = -1.0
+    return result.reshape(12 * rows, 96)
+
+
 def volume_table(count, width):
     table = diff_table(fine_points() if count == 5 else np.array([-1.0, 0.0, 1.0]))
     unit = np.eye(count)
@@ -104,15 +131,20 @@
     for n, (a, b, c) in enumerate(itertools.product(range(3), repeat=3)):
         pick[n, (2 * a * 5 + 2 * b) * 5 + 2 * c] = 1.0
     restrict = padded(triple(prolong.T, prolong.T, prolong.T), 32, 128)
-    restrict = np.concatenate([restrict, take_c @ restrict])
+    restrict = np.concatenate([restrict, take_c @ restrict, line_table(3, 32) @ restrict])
     extend = padded(triple(prolong, prolong, prolong), 128, 32)
     flat = np.kron(prolong, prolong)
     flat = np.concatenate([flat, np.repeat(flat[24:25], 7, axis=0)])
     face_extend = np.zeros((192, 96))
     for face in range(6):
         face_extend[32 * face : 32 * face + 32, 16 * face : 16 * face + 9] = flat
+    face_pick = np.zeros((96, 192))
+    for face in range(6):
+        for row in range(16):
+            a, b = divmod(min(row, 8), 3)
+            face_pick[16 * face + row, 32 * face + 10 * a + 2 * b] = 1.0
     return {
-        "take": two(np.concatenate([take, pick, take_c @ pick])),
+        "take": two(np.concatenate([take, line_table(5, 128), pick])),
         "volume": three(volume_table(5, 128)),
         "give": two(-FINE_FACE * np.concatenate([take @ give, give])),
         "restrict": three(restrict),
@@ -121,6 +153,9 @@
         "give_c": two(-COARSE_FACE * np.concatenate([take_c @ give_c, give_c])),
         "extend": three(extend),
         "face_extend": three(face_extend),
+        "lines": two(line_faces(5, 32)),
+        "lines_c": two(line_faces(3, 16)),
+        "pick_face": two(face_pick),
     }
 
 
@@ -200,19 +235,28 @@
 
 
 def kernel(start_h, source_h, density_h, velocity_h, pressure_h, shift_h, inverse_h, *rest):
-    tables_h, rest = rest[:9], rest[9:]
+    tables_h, rest = rest[:12], rest[12:]
     out_h, rest = rest[0], rest[1:]
     (start_r, source_r, density_r, velocity_r, pressure_r, shift_r, inverse_r), rest = rest[:7], rest[7:]
-    tables_r, rest = rest[:9], rest[9:]
-    (take, volume, give, restrict, restrict_give, volume_c, give_c, extend, face_extend) = tables_r
+    tables_r, rest = rest[:12], rest[12:]
+    (
+        take, volume, give, restrict, restrict_give, volume_c, give_c, extend, face_extend,
+        lines, lines_c, pick_face,
+    ) = tables_r
     (
         field, source, state, base, split_n, cot,
-        face_state, face_field, jump, split_f, compact, own,
+        face_state, start_face, face_field, jump, split_f, compact, own,
+        near_state, near, across, line_field, split_l, near_blocks, block_row, edges, signs, signs_c,
         state_c, field_c, base_c, split_c, split_cf, cot_c, jump_c, compact_c, own_c,
+        near_state_c, near_c, across_c, face_c,
         blocks, shift, out_r,
-    ), rest = rest[:24], rest[24:]
-    send_fine, recv_fine, send_coarse, recv_coarse, rest = rest[:6], rest[6:12], rest[12:18], rest[18:24], rest[24:]
-    in_sems, out_sem, send_sems, recv_sems = rest
+    ), rest = rest[:39], rest[39:]
+    kinds = []
+    for _ in range(5):
+        kinds.append((rest[:6], rest[6:12]))
+        rest = rest[12:]
+    fine_u, fine_t, fine_w, coarse_u, coarse_w = kinds
+    send_lines, recv_lines, in_sems, out_sem, send_sems, recv_sems, send_line_sems, recv_line_sems = rest
 
     place = [lax.axis_index(axis) for axis in AXES]
     size = [lax.axis_size(axis) for axis in AXES]
@@ -221,6 +265,15 @@
     def partner(f):
         target = list(place)
         target[f // 2] = target[f // 2] + (1 if f % 2 else -1)
+        return tuple(target)
+
+    both = [has[2 * i + s] & has[2 * j + t] for i, j, s, t in LINES]
+
+    def line_partner(line):
+        i, j, s, t = LINES[line]
+        target = list(place)
+        target[i] = target[i] + 2 * s - 1
+        target[j] = target[j] + 2 * t - 1
         return tuple(target)
 
     barrier = pltpu.get_barrier_semaphore()
@@ -228,6 +281,10 @@
         @pl.when(has[f])
         def _(f=f):
             pl.semaphore_signal(barrier, inc=1, device_id=partner(f), device_id_type=MESH)
+    for line in range(12):
+        @pl.when(both[line])
+        def _(line=line):
+            pl.semaphore_signal(barrier, inc=1, device_id=line_partner(line), device_id_type=MESH)
 
     field[120:128, :] = jnp.zeros((8, 640), F32)
     source[120:128, :] = jnp.zeros((8, 640), F32)
@@ -235,7 +292,7 @@
         (start_h, start_r), (tables_h[0], take), (velocity_h, velocity_r), (density_h, density_r),
         (pressure_h, pressure_r), (tables_h[1], volume), (source_h, source_r), (shift_h, shift_r),
         (inverse_h, inverse_r), (tables_h[2], give),
-    ] + [(tables_h[n], tables_r[n]) for n in range(3, 9)]
+    ] + [(tables_h[n], tables_r[n]) for n in range(3, 12)]
     inward = [pltpu.make_async_copy(a, b, in_sems.at[n]) for n, (a, b) in enumerate(order)]
     for copy in inward:
         copy.start()
@@ -280,37 +337,119 @@
         amount %= 128
         return pltpu.roll(value, amount, 1) if amount else value
 
-    def copies(exchange, sends, receives):
-        row = exchange + (2 if sends is send_coarse else 0)
+    def copies(kind):
+        sends, receives = kinds[kind]
         return [
             pltpu.make_async_remote_copy(
-                src_ref=sends[f].at[exchange],
-                dst_ref=receives[f ^ 1].at[exchange],
-                send_sem=send_sems.at[row, f],
-                recv_sem=recv_sems.at[row, f ^ 1],
+                src_ref=sends[f],
+                dst_ref=receives[f ^ 1],
+                send_sem=send_sems.at[kind, f],
+                recv_sem=recv_sems.at[kind, f ^ 1],
                 device_id=partner(f),
                 device_id_type=MESH,
             )
             for f in range(6)
         ]
 
-    def send(exchange, faces, sends, remote):
+    def line_copies(level):
+        return [
+            pltpu.make_async_remote_copy(
+                src_ref=send_lines.at[level, line],
+                dst_ref=recv_lines.at[level, line ^ 3],
+                send_sem=send_line_sems.at[level, line],
+                recv_sem=recv_line_sems.at[level, line ^ 3],
+                device_id=line_partner(line),
+                device_id_type=MESH,
+            )
+            for line in range(12)
+        ]
+
+    remote = [copies(kind) for kind in range(5)]
+    remote_lines = [line_copies(level) for level in range(2)]
+
+    def pack(kind, read, height, top=0, slots=None):
         for f in range(6):
             dim, side = divmod(f, 2)
             count, stride = COUNTS[dim], STRIDES[dim]
-            slot = sends[f].shape[1]
+            target = kinds[kind][0][f]
+            slot = target.shape[0] if slots is None else slots[dim]
             where = lane_place(slot, dim)
             packed = None
-            for g in range(faces.shape[1] // slot):
-                block = turn(faces[f, g * slot : g * slot + slot, :], (g - side * (count - 1)) * stride)
+            for g in range(height // slot):
+                block = turn(read(f, g * slot, slot), (g - side * (count - 1)) * stride)
                 packed = block if packed is None else jnp.where(where == g, block, packed)
-            sends[f][exchange] = packed
-            if exchange == 0 and sends is send_fine and f == 0:
-                pl.semaphore_wait(barrier, sum(h.astype(jnp.int32) for h in has))
-
+            first = top if slots is None else top[dim]
+            target[first : first + slot, :] = packed
+
+    def pack_lines(level, source_ref, offset):
+        for line, (i, j, s, t) in enumerate(LINES):
+            where = lane_place(8, j)
+            packed = None
+            for v in range(5):
+                block = source_ref[offset + 8 * line : offset + 8 * line + 8, lanes(v)]
+                block = turn(block, (v - t * (COUNTS[j] - 1)) * STRIDES[j])
+                packed = block if packed is None else jnp.where(where == v, block, packed)
+            send_lines[level, line] = packed
+
+    def start(kind):
+        for f in range(6):
             @pl.when(has[f])
+            def _(f=f):
+                remote[kind][f].start()
+
+    def start_lines(level):
+        for line in range(12):
+            @pl.when(both[line])
+            def _(line=line):
+                remote_lines[level][line].start()
+
+    def unpack(kind, f, height, write, sign=1.0, top=0, slots=None):
+        dim, side = divmod(f, 2)
+        count, stride = COUNTS[dim], STRIDES[dim]
+        received = kinds[kind][1][f]
+        slot = received.shape[0] if slots is None else slots[dim]
+        first = top if slots is None else top[dim]
+        edge = jnp.where(lane_place(slot, dim) == side * (count - 1), sign, 0.0)
+
+        @pl.when(has[f])
+        def _():
+            packed = received[first : first + slot, :]
+            for g in range(height // slot):
+                write(f, g * slot, slot, edge * turn(packed, (side * (count - 1) - g) * stride))
+
+        @pl.when(jnp.logical_not(has[f]))
+        def _():
+            write(f, 0, height, jnp.zeros((height, 128), F32))
+
+    def arrive(kind, f):
+        @pl.when(has[f])
+        def _():
+            remote[kind][f ^ 1].wait_recv()
+
+    def receive(kind, target, sign):
+        def write(f, first, slot, value):
+            target[f, first : first + slot, :] = value
+
+        for f in range(6):
+            arrive(kind, f)
+            unpack(kind, f, target.shape[1], write, sign)
+
+    def receive_lines(level, target):
+        for line, (i, j, s, t) in enumerate(LINES):
+            edge = (lane_place(8, i) == s * (COUNTS[i] - 1)) & (lane_place(8, j) == t * (COUNTS[j] - 1))
+            here = slice(8 * line, 8 * line + 8)
+
+            @pl.when(both[line])
             def _():
-                remote[f].start()
+                remote_lines[level][line ^ 3].wait_recv()
+                packed = recv_lines[level, line]
+                for v in range(5):
+                    amount = (t * (COUNTS[j] - 1) - v) * STRIDES[j] + (2 * s - 1) * (COUNTS[i] - 1) * STRIDES[i]
+                    target[here, lanes(v)] = jnp.where(edge, turn(packed, amount), 0.0)
+
+            @pl.when(jnp.logical_not(both[line]))
+            def _():
+                target[here, :] = jnp.zeros((8, 640), F32)
 
     def own_part(faces, result):
         for f in range(6):
@@ -319,26 +458,6 @@
             inside = lane_place(faces.shape[1], dim) != side * (count - 1)
             other = turn(faces[f ^ 1], -stride if side else stride)
             result[f] = faces[f] - jnp.where(inside, other, 0.0)
-
-    def receive(exchange, receives, remote, result, target):
-        for f in range(6):
-            dim, side = divmod(f, 2)
-            count, stride = COUNTS[dim], STRIDES[dim]
-            slot = receives[f].shape[1]
-            edge = lane_place(slot, dim) == side * (count - 1)
-
-            @pl.when(has[f])
-            def _():
-                remote[f ^ 1].wait_recv()
-                packed = receives[f][exchange]
-                for g in range(result.shape[1] // slot):
-                    here = slice(g * slot, g * slot + slot)
-                    there = turn(packed, (side * (count - 1) - g) * stride)
-                    target[f, here, :] = result[f, here, :] - jnp.where(edge, there, 0.0)
-
-            @pl.when(jnp.logical_not(has[f]))
-            def _():
-                target[f] = result[f]
 
     def face_pull(step, values, state_ref, offset, per_face):
         f = lax.div(step, per_face)
@@ -351,9 +470,51 @@
         normal = pick[0] * values[1] + pick[1] * values[2] + pick[2] * values[3]
         return pull_face(values, local, speed, normal, pick, sign)
 
+    def neighbour(rows, face, mine, offset, near_s, across_ref, sign_ref, near_ref, target):
+        per_face = rows // 16
+        for d in range(3):
+            p, q = [n for n in range(3) if n != d]
+
+            def one(step, _, d=d, p=p, q=q):
+                side = lax.div(step, per_face)
+                f = 2 * d + side
+                at = step + 2 * d * per_face
+                here = rows_of(at)
+                local = load(near_s, here)
+                top = [jnp.abs(local[n]) + local[4] for n in range(3)]
+                edge = edges[f]
+                own_side = load(mine, rows_of(at + offset))
+                jumps = [None] * 3
+                jumps[d] = [-edge * value for value in own_side]
+                jumps[p] = load(across_ref, here)
+                jumps[q] = load(across_ref, rows_of(at + 6 * per_face))
+                part = rows_of(step - side * per_face)
+                sign = [None] * 3
+                sign[d] = (1 - 2 * side).astype(F32)
+                sign[p], sign[q] = sign_ref[0, part, :], sign_ref[1, part, :]
+                pulled = pull_all([[sign[n] * value for value in jumps[n]] for n in range(3)], local)
+                for n in range(3):
+                    pulled = [pulled[v] + top[n] * jumps[n][v] for v in range(5)]
+                inverse = [near_blocks[f, pl.ds(n, 1), :] for n in range(25)]
+                change = apply_blocks(inverse, pulled)
+                old = load(near_ref, here)
+                jumps_now = load(target, here)
+                store(target, here, [jumps_now[v] - (old[v] - face * change[v]) for v in range(5)])
+                return 0
+
+            lax.fori_loop(0, 2 * per_face, one, 0)
+
     def block_rows():
         return [blocks[n] for n in range(25)]
 
+    for f in range(6):
+        dim, side = divmod(f, 2)
+        edges[f] = (lane_place(16, dim) == side * (COUNTS[dim] - 1)).astype(F32)
+    for ref, rows, count in ((signs, 32, 5), (signs_c, 16, 3)):
+        row = jnp.minimum(lax.broadcasted_iota(jnp.int32, (rows, 128), 0), count * count - 1)
+        for n, at in enumerate((row // count, row % count)):
+            ref[n] = jnp.where(at == 0, -1.0, jnp.where(at == count - 1, 1.0, 0.0))
+    block_row[...] = jnp.zeros((32, 128), F32)
     inward[0].wait()
     for v in range(5):
         field[0:125, lanes(v)] = start_r[v]
@@ -364,10 +525,13 @@
 
     lax.fori_loop(0, 8, split_field, 0)
     inward[1].wait()
-    face_field[...] = dot(take[0:192, :], split_n[0:256, :])
-    gather_faces(face_field, 0, 32, 24, compact)
-    fine_0 = copies(0, send_fine, recv_fine)
-    send(0, compact, send_fine, fine_0)
+    start_face[...] = dot(take[0:192, :], split_n[0:256, :])
+    line_field[...] = dot(take[192:288, :], split_n[0:256, :])
+    gather_faces(start_face, 0, 32, 24, compact)
+    pack(0, lambda f, first, slot: compact[f, first : first + slot, :], 128)
+    pack_lines(0, line_field, 0)
+    own_part(compact, own)
+    scatter_faces(own, 32, 24, jump)
 
     for n in (2, 3, 4):
         inward[n].wait()
@@ -387,8 +551,7 @@
 
     lax.fori_loop(0, 8, split_state, 0)
     face_state[...] = dot(take[0:192, :], split_f[0:256, :])
-    state_c[...] = dot(take[192:320, :], split_f[0:256, :])
-    own_part(compact, own)
+    state_c[0:32, :] = dot(take[288:320, :], split_f[0:256, :])
 
     for n in (7, 8):
         inward[n].wait()
@@ -409,6 +572,14 @@
     shift[...] = to_lanes(shift_r[...], 1)[0]
     blocks[...] = OMEGA * to_lanes(inverse_r[...], 25)
 
+    for n in range(25):
+        block_row[n : n + 1, :] = blocks[n, 0:1, :]
+    gather_faces(face_state, 0, 32, 24, compact)
+    slots, tops = (64, 16, 16), (0, 0, 0)
+    pack(1, lambda f, first, slot: compact[f, first : first + slot, :], 128, tops, slots)
+    block_slots, block_tops = (16, 8, 8), (64, 16, 16)
+    pack(1, lambda f, first, slot: block_row[first : first + slot, :], 32, block_tops, block_slots)
+
     inward[5].wait()
     inward[6].wait()
     for v in range(5):
@@ -433,6 +604,10 @@
 
     cot[...] = dot(volume[...], split_n[...])
     lax.fori_loop(0, 8, lambda s, c: smooth_volume(s, c, True), 0)
+    pl.semaphore_wait(barrier, sum(h.astype(jnp.int32) for h in has + both))
+    start(0)
+    start(1)
+    start_lines(0)
     face_field[...] = dot(take[0:192, :], split_n[0:256, :])
 
     def smooth_faces(step, _):
@@ -440,19 +615,34 @@
         store_split(split_f, step, 192, apply_blocks(block_rows(), values), 2)
         return 0
 
-    receive(0, recv_fine, fine_0, own, compact)
-    scatter_faces(compact, 32, 24, jump)
     lax.fori_loop(0, 12, smooth_faces, 0)
     inward[9].wait()
     face_field[...] += dot(give[0:192, :], split_f[0:384, :])
     gather_faces(face_field, 0, 32, 24, compact)
-    fine_1 = copies(1, send_fine, recv_fine)
-    send(1, compact, send_fine, fine_1)
-
-    for n in range(10, 16):
+    pack(2, lambda f, first, slot: compact[f, first : first + slot, :], 128)
+    start(2)
+    base[...] += dot(give[192:320, :], split_f[0:384, :])
+    for n in range(10, 19):
         inward[n].wait()
+
+    def split_faces(step, ref):
+        store_split(split_f, step, 192, load(ref, rows_of(step)), 2)
+
+    def split_face_state(step, _):
+        split_faces(step, face_state)
+        return 0
+
+    lax.fori_loop(0, 12, split_face_state, 0)
+    state_c[32:128, :] = dot(pick_face[...], split_f[0:384, :])
+
+    receive(0, compact, -1.0)
+    scatter_faces(compact, 32, 24, jump)
+    lax.fori_loop(0, 12, smooth_faces, 0)
+    face_field[...] += dot(give[0:192, :], split_f[0:384, :])
     field[...] = base[...] + dot(give[192:320, :], split_f[0:384, :])
+    gather_faces(face_field, 0, 32, 24, compact)
     own_part(compact, own)
+    scatter_faces(own, 32, 24, jump)
     lax.fori_loop(0, 8, split_field, 0)
     cot[...] = dot(volume[...], split_n[...])
 
@@ -465,13 +655,34 @@
     lax.fori_loop(0, 8, residual_volume, 0)
     field_c[...] = dot(restrict[...], split_n[...])
 
+    def write_state(f, first, slot, value):
+        compact[f, first : first + slot, :] = value
+
+    def write_blocks(f, first, slot, value):
+        near_blocks[f, first : first + slot, :] = value
+
+    for f in range(6):
+        arrive(1, f)
+        unpack(1, f, 128, write_state, 1.0, tops, slots)
+        unpack(1, f, 32, write_blocks, 1.0, block_tops, block_slots)
+    scatter_faces(compact, 32, 24, near_state)
+    receive_lines(0, line_field)
+
+    def split_lines(step, _):
+        store_split(split_l, step, 96, load(line_field, rows_of(step)), 2)
+        return 0
+
+    lax.fori_loop(0, 6, split_lines, 0)
+    across[...] = dot(lines[...], split_l[...])
+    receive(2, compact, 1.0)
+    scatter_faces(compact, 32, 24, near)
+    neighbour(32, FINE_FACE, start_face, 0, near_state, across, signs, near, jump)
+
     def residual_faces(step, _):
         values = face_pull(step, load(jump, rows_of(step)), face_state, 0, 2)
         store_split(split_f, step, 192, values, 3)
         return 0
 
-    receive(1, recv_fine, fine_1, own, compact)
-    scatter_faces(compact, 32, 24, jump)
     lax.fori_loop(0, 12, residual_faces, 0)
     field_c[...] += dot(restrict_give[...], split_f[...])
 
@@ -480,11 +691,14 @@
         store(base_c, rows, apply_blocks(block_rows(), load(field_c, rows)))
         return 0
 
-    lax.fori_loop(0, 8, coarse_first, 0)
+    lax.fori_loop(0, 14, coarse_first, 0)
     gather_faces(base_c, 32, 16, 8, compact_c)
-    coarse_0 = copies(0, send_coarse, recv_coarse)
-    send(0, compact_c, send_coarse, coarse_0)
+    pack(3, lambda f, first, slot: compact_c[f, first : first + slot, :], 48)
+    start(3)
+    pack_lines(1, base_c, 128)
+    start_lines(1)
     own_part(compact_c, own_c)
+    scatter_faces(own_c, 16, 8, jump_c)
 
     def split_coarse(step, _):
         store_split(split_c, step, 32, load(base_c, rows_of(step)), 2)
@@ -504,26 +718,38 @@
         return 0
 
     lax.fori_loop(0, 2, coarse_volume, 0)
-    base_c[32:128, :] = dot(volume_c[96:192, :], split_c[0:64, :])
+    face_c[...] = dot(volume_c[96:192, :], split_c[0:64, :])
 
     def coarse_faces(step, _):
         values = face_pull(step, load(jump_c, rows_of(step)), state_c, 2, 1)
         store_split(split_cf, step, 96, apply_blocks(block_rows(), values), 2)
         return 0
 
-    receive(0, recv_coarse, coarse_0, own_c, compact_c)
+    lax.fori_loop(0, 6, coarse_faces, 0)
+    face_c[...] += dot(give_c[0:96, :], split_cf[0:192, :])
+    gather_faces(face_c, 0, 16, 8, compact_c)
+    pack(4, lambda f, first, slot: compact_c[f, first : first + slot, :], 48)
+    start(4)
+    field_c[0:32, :] += dot(give_c[96:128, :], split_cf[0:192, :])
+
+    def split_near(step, _):
+        split_faces(step, near_state)
+        return 0
+
+    lax.fori_loop(0, 12, split_near, 0)
+    near_state_c[...] = dot(pick_face[...], split_f[0:384, :])
+
+    receive(3, compact_c, -1.0)
     scatter_faces(compact_c, 16, 8, jump_c)
     lax.fori_loop(0, 6, coarse_faces, 0)
-    base_c[32:128, :] += dot(give_c[0:96, :], split_cf[0:192, :])
-    gather_faces(base_c, 32, 16, 8, compact_c)
-    coarse_1 = copies(1, send_coarse, recv_coarse)
-    send(1, compact_c, send_coarse, coarse_1)
-
-    base_c[0:32, :] = field_c[0:32, :] + dot(give_c[96:128, :], split_cf[0:192, :])
+    face_c[...] += dot(give_c[0:96, :], split_cf[0:192, :])
+    field_c[0:32, :] += dot(give_c[96:128, :], split_cf[0:192, :])
+    gather_faces(face_c, 0, 16, 8, compact_c)
     own_part(compact_c, own_c)
+    scatter_faces(own_c, 16, 8, jump_c)
 
     def split_coarse_3(step, _):
-        store_split(split_c, step, 32, load(base_c, rows_of(step)), 3)
+        store_split(split_c, step, 32, load(field_c, rows_of(step)), 3)
         return 0
 
     lax.fori_loop(0, 2, split_coarse_3, 0)
@@ -531,13 +757,17 @@
     lax.fori_loop(0, 8, split_field, 0)
     cot[...] = dot(volume[...], split_n[...])
     lax.fori_loop(0, 8, lambda s, c: smooth_volume(s, c, False), 0)
+    receive_lines(1, line_field)
+    lax.fori_loop(0, 6, split_lines, 0)
+    across_c[...] = dot(lines_c[...], split_l[...])
+    receive(4, compact_c, 1.0)
+    scatter_faces(compact_c, 16, 8, near_c)
+    neighbour(16, COARSE_FACE, base_c, 2, near_state_c, across_c, signs_c, near_c, jump_c)
 
     def split_jump(step, _):
         store_split(split_cf, step, 96, load(jump_c, rows_of(step)), 3)
         return 0
 
-    receive(1, recv_coarse, coarse_1, own_c, compact_c)
-    scatter_faces(compact_c, 16, 8, jump_c)
     lax.fori_loop(0, 6, split_jump, 0)
     jump[...] += dot(face_extend[...], split_cf[...])
     lax.fori_loop(0, 12, smooth_faces, 0)
@@ -546,11 +776,16 @@
         out_r[v] = base[0:125, lanes(v)]
     outward = pltpu.make_async_copy(out_r, out_h, out_sem)
     outward.start()
-    for n, remote in enumerate((fine_0, fine_1, coarse_0, coarse_1)):
+    for kind in range(5):
         for f in range(6):
             @pl.when(has[f])
-            def _(remote=remote, f=f):
-                remote[f].wait_send()
+            def _(kind=kind, f=f):
+                remote[kind][f].wait_send()
+    for level in range(2):
+        for line in range(12):
+            @pl.when(both[line])
+            def _(level=level, line=line):
+                remote_lines[level][line].wait_send()
     outward.wait()
 
 
@@ -562,20 +797,28 @@
     work = [
         vmem((128, 640), F32), vmem((128, 640), F32), vmem((128, 640), F32), vmem((128, 640), F32),
         vmem((384, 640), BF16), vmem((384, 640), F32),
-        vmem((192, 640), F32), vmem((192, 640), F32), vmem((192, 640), F32), vmem((576, 640), BF16),
-        vmem((6, 128, 128), F32), vmem((6, 128, 128), F32),
-        vmem((128, 640), F32), vmem((128, 640), F32), vmem((128, 640), F32), vmem((96, 640), BF16),
+        vmem((192, 640), F32), vmem((192, 640), F32), vmem((192, 640), F32), vmem((192, 640), F32),
+        vmem((576, 640), BF16), vmem((6, 128, 128), F32), vmem((6, 128, 128), F32),
+        vmem((192, 640), F32), vmem((192, 640), F32), vmem((384, 640), F32), vmem((96, 640), F32),
+        vmem((192, 640), BF16), vmem((6, 32, 128), F32), vmem((32, 128), F32), vmem((6, 16, 128), F32),
+        vmem((2, 32, 128), F32), vmem((2, 16, 128), F32),
+        vmem((128, 640), F32), vmem((224, 640), F32), vmem((224, 640), F32), vmem((96, 640), BF16),
         vmem((288, 640), BF16), vmem((96, 640), F32), vmem((96, 640), F32),
         vmem((6, 48, 128), F32), vmem((6, 48, 128), F32),
+        vmem((96, 640), F32), vmem((96, 640), F32), vmem((192, 640), F32), vmem((96, 640), F32),
         vmem((25, 16, 128), F32), vmem((16, 128), F32), vmem(args[0].shape, F32),
     ]
-    fine = [vmem((2, rows, 128), F32) for rows in (64, 64, 16, 16, 16, 16)]
-    coarse = [vmem((2, rows, 128), F32) for rows in (24, 24, 8, 8, 8, 8)]
+    fine = [vmem((rows, 128), F32) for rows in (64, 64, 16, 16, 16, 16)]
+    static = [vmem((rows, 128), F32) for rows in (80, 80, 24, 24, 24, 24)]
+    coarse = [vmem((rows, 128), F32) for rows in (24, 24, 8, 8, 8, 8)]
+    kinds = [*fine, *fine, *static, *static, *fine, *fine, *coarse, *coarse, *coarse, *coarse]
     sems = [
-        pltpu.SemaphoreType.DMA((16,)),
+        pltpu.SemaphoreType.DMA((19,)),
         pltpu.SemaphoreType.DMA,
-        pltpu.SemaphoreType.DMA((4, 6)),
-        pltpu.SemaphoreType.DMA((4, 6)),
+        pltpu.SemaphoreType.DMA((5, 6)),
+        pltpu.SemaphoreType.DMA((5, 6)),
+        pltpu.SemaphoreType.DMA((2, 12)),
+        pltpu.SemaphoreType.DMA((2, 12)),
     ]
     anywhere = pl.BlockSpec(memory_space=pl.ANY)
     return pl.pallas_call(
@@ -583,7 +826,7 @@
         out_shape=jax.ShapeDtypeStruct(args[0].shape, F32),
         in_specs=[anywhere] * (len(args) + len(constants)),
         out_specs=anywhere,
-        scratch_shapes=raw + held + work + fine + fine + coarse + coarse + sems,
+        scratch_shapes=raw + held + work + kinds + [vmem((2, 12, 8, 128), F32)] * 2 + sems,
         compiler_params=pltpu.CompilerParams(
             collective_id=0, has_side_effects=True, vmem_limit_bytes=60 * 1024 * 1024
         ),

time: 37.9 us -> 35.7 us (0.942)
  Pallas kernels: 36.1 us -> 33.8 us
    pallas_call x1, Pallas kernels: 36.1 us -> 33.8 us  [body(): pl.pallas_call(kernel, out_shape=jax.ShapeDtypeStruct(args[0].shape, F32)...]
where the time goes in v2:
time: 35.7 us; the launch traced here: 35.6 us
  Pallas kernels  33.8 us (95%)
  local copies, waits for them, and re-layouts  1.72 us (5%)
    pallas_call x1, Pallas kernels, body(): pl.pallas_call(kernel, out_shape=jax.ShapeDtypeStruct(args[0].shape, F32)...  33.8 us
    unnamed x1, local copies, waits for them, and re-layouts  1.72 us

profile of v2, /device:TPU:30, one launch (start us, length us, event | category | flops | bytes accessed | tf_op | source)
XLA Modules:
  0.0 35.6 jit_solution(13261722261211399221)
XLA Ops:
  0.0 33.8 %shard_map.181 = f32[5,125,128]{2,1,0:T(8,128)} custom-call(f32[5,125,128]{2,1,0:T(8,128)} %start_h.1, f32[5,125,128]{2,1,0:T(8,128)} %source_h.1, f32[125,128]{1,0:T(8,128)} %density_h.1, f32[3,125,128]{2,1,0:T(8,128)} %velocity_h.1, f32[125,128]{1,0:T(8,128)} %pressure_h.1, f32[2,8,8]{2,1,0:T(8,128)} %shift_h.1, f32[5,5,2,8,8]{4,3,2,1,0:T(8,128)} %inverse_h.1, ...), custom_call_target="tpu_custom_call" | custom-call | tf_op jit(solution)/shard_map/pallas_call | solution.py:824
  33.8 1.7 %copy.21 = f32[5,125,128]{2,1,0:T(8,128)} copy(f32[5,125,128]{2,1,0:T(8,128)} %shard_map.181) | data formatting | bytes 640000

commit v3 on v2

--- a/solution.py
+++ b/solution.py
@@ -173,8 +173,13 @@
     return slice(128 * var, 128 * var + 128)
 
 
+def steps(count, one, carry):
+    for step in range(count):
+        one(step, carry)
+
+
 def rows_of(step, size=16):
-    return pl.ds(pl.multiple_of(step * size, size), size)
+    return slice(step * size, step * size + size)
 
 
 def load(ref, rows):
@@ -209,19 +214,21 @@
     return [first, *middle, total + energy]
 
 
-def pull_face(jump, state, speed, normal, pick, sign):
+def pull_face(jump, state, d, sign):
     w = state[:3]
     crossed = w[0] * jump[1] + w[1] * jump[2] + w[2] * jump[3] + state[3] * jump[4]
-    end = speed * jump[4]
-    total = 0.4 * (normal + end)
+    end = w[d] * jump[4]
+    total = 0.4 * (jump[1 + d] + end)
     half_square = 0.5 * (w[0] * w[0] + w[1] * w[1] + w[2] * w[2])
-    turned = jump[0] + crossed
-    out = [half_square * total - speed * crossed]
+    out = [half_square * total - w[d] * crossed]
     for j in range(3):
-        out.append(speed * jump[1 + j] - w[j] * total + pick[j] * turned)
+        out.append(w[d] * jump[1 + j] - w[j] * total)
+    out[1 + d] = out[1 + d] + (jump[0] + crossed)
     out.append(total + end)
-    top = jnp.abs(speed) + state[4]
-    return [sign * out[v] + top * jump[v] for v in range(5)]
+    top = jnp.abs(w[d]) + state[4]
+    if sign > 0:
+        return [top * jump[v] + out[v] for v in range(5)]
+    return [top * jump[v] - out[v] for v in range(5)]
 
 
 def apply_blocks(blocks, values):
@@ -246,17 +253,17 @@
     (
         field, source, state, base, split_n, cot,
         face_state, start_face, face_field, jump, split_f, compact, own,
-        near_state, near, across, line_field, split_l, near_blocks, block_row, edges, signs, signs_c,
+        near_state, across, line_field, split_l, near_blocks, block_row, edges, signs, signs_c,
         state_c, field_c, base_c, split_c, split_cf, cot_c, jump_c, compact_c, own_c,
-        near_state_c, near_c, across_c, face_c,
-        blocks, shift, out_r,
-    ), rest = rest[:39], rest[39:]
+        near_state_c, across_c, face_c,
+        blocks, shift,
+    ), rest = rest[:36], rest[36:]
     kinds = []
     for _ in range(5):
         kinds.append((rest[:6], rest[6:12]))
         rest = rest[12:]
     fine_u, fine_t, fine_w, coarse_u, coarse_w = kinds
-    send_lines, recv_lines, in_sems, out_sem, send_sems, recv_sems, send_line_sems, recv_line_sems = rest
+    send_lines, recv_lines, in_sems, send_sems, recv_sems, send_line_sems, recv_line_sems = rest
 
     place = [lax.axis_index(axis) for axis in AXES]
     size = [lax.axis_size(axis) for axis in AXES]
@@ -306,32 +313,32 @@
 
         def one(f, _):
             top = offset + f * rows
-            last = source_ref[pl.ds(pl.multiple_of(top + whole, 8), 8), lanes(0)]
+            last = source_ref[slice(top + whole, top + whole + 8), lanes(0)]
             for v in range(5):
                 target[f, whole * v : whole * v + whole, :] = source_ref[
-                    pl.ds(pl.multiple_of(top, 8), whole), lanes(v)
+                    slice(top, top + whole), lanes(v)
                 ]
                 if v:
-                    here = source_ref[pl.ds(pl.multiple_of(top + whole, 8), 8), lanes(v)]
+                    here = source_ref[slice(top + whole, top + whole + 8), lanes(v)]
                     last = jnp.where(sub == v, here, last)
             target[f, 5 * whole : 5 * whole + 8, :] = last
             return 0
 
-        lax.fori_loop(0, 6, one, 0)
-
-    def scatter_faces(source_ref, rows, whole, target):
+        steps(6, one, 0)
+
+    def scatter_faces(source_ref, rows, whole, target, add=False):
+        def put(here, v, value):
+            target[here, lanes(v)] = target[here, lanes(v)] + value if add else value
+
         def one(f, _):
             top = f * rows
             for v in range(5):
-                target[pl.ds(pl.multiple_of(top, 8), whole), lanes(v)] = source_ref[
-                    f, whole * v : whole * v + whole, :
-                ]
-                target[pl.ds(pl.multiple_of(top + whole, 8), 8), lanes(v)] = jnp.broadcast_to(
-                    source_ref[f, pl.ds(5 * whole + v, 1), :], (8, 128)
-                )
+                put(slice(top, top + whole), v, source_ref[f, whole * v : whole * v + whole, :])
+                last = source_ref[f, 5 * whole + v : 5 * whole + v + 1, :]
+                put(slice(top + whole, top + whole + 8), v, jnp.broadcast_to(last, (8, 128)))
             return 0
 
-        lax.fori_loop(0, 6, one, 0)
+        steps(6, one, 0)
 
     def turn(value, amount):
         amount %= 128
@@ -460,23 +467,16 @@
             result[f] = faces[f] - jnp.where(inside, other, 0.0)
 
     def face_pull(step, values, state_ref, offset, per_face):
-        f = lax.div(step, per_face)
-        d = lax.div(f, 2)
-        sign = (2 * (f - 2 * d) - 1).astype(F32)
-        pick = [(d == j).astype(F32) for j in range(3)]
-        rows = rows_of(step + offset)
-        local = load(state_ref, rows)
-        speed = state_ref[rows, pl.ds(pl.multiple_of(d * 128, 128), 128)]
-        normal = pick[0] * values[1] + pick[1] * values[2] + pick[2] * values[3]
-        return pull_face(values, local, speed, normal, pick, sign)
-
-    def neighbour(rows, face, mine, offset, near_s, across_ref, sign_ref, near_ref, target):
+        d, side = divmod(step // per_face, 2)
+        return pull_face(values, load(state_ref, rows_of(step + offset)), d, 2 * side - 1)
+
+    def neighbour(rows, face, mine, offset, near_s, across_ref, sign_ref, target):
         per_face = rows // 16
         for d in range(3):
             p, q = [n for n in range(3) if n != d]
 
             def one(step, _, d=d, p=p, q=q):
-                side = lax.div(step, per_face)
+                side = step // per_face
                 f = 2 * d + side
                 at = step + 2 * d * per_face
                 here = rows_of(at)
@@ -490,19 +490,18 @@
                 jumps[q] = load(across_ref, rows_of(at + 6 * per_face))
                 part = rows_of(step - side * per_face)
                 sign = [None] * 3
-                sign[d] = (1 - 2 * side).astype(F32)
+                sign[d] = 1.0 - 2.0 * side
                 sign[p], sign[q] = sign_ref[0, part, :], sign_ref[1, part, :]
                 pulled = pull_all([[sign[n] * value for value in jumps[n]] for n in range(3)], local)
                 for n in range(3):
                     pulled = [pulled[v] + top[n] * jumps[n][v] for v in range(5)]
-                inverse = [near_blocks[f, pl.ds(n, 1), :] for n in range(25)]
+                inverse = [near_blocks[f, n : n + 1, :] for n in range(25)]
                 change = apply_blocks(inverse, pulled)
-                old = load(near_ref, here)
                 jumps_now = load(target, here)
-                store(target, here, [jumps_now[v] - (old[v] - face * change[v]) for v in range(5)])
+                store(target, here, [jumps_now[v] + face * change[v] for v in range(5)])
                 return 0
 
-            lax.fori_loop(0, 2 * per_face, one, 0)
+            steps(2 * per_face, one, 0)
 
     def block_rows():
         return [blocks[n] for n in range(25)]
@@ -523,7 +522,7 @@
         store_split(split_n, step, 128, load(field, rows_of(step)), 3)
         return 0
 
-    lax.fori_loop(0, 8, split_field, 0)
+    steps(8, split_field, 0)
     inward[1].wait()
     start_face[...] = dot(take[0:192, :], split_n[0:256, :])
     line_field[...] = dot(take[192:288, :], split_n[0:256, :])
@@ -549,7 +548,7 @@
         store_split(split_f, step, 128, load(state, rows_of(step)), 2)
         return 0
 
-    lax.fori_loop(0, 8, split_state, 0)
+    steps(8, split_state, 0)
     face_state[...] = dot(take[0:192, :], split_f[0:256, :])
     state_c[0:32, :] = dot(take[288:320, :], split_f[0:256, :])
 
@@ -603,7 +602,7 @@
         return 0
 
     cot[...] = dot(volume[...], split_n[...])
-    lax.fori_loop(0, 8, lambda s, c: smooth_volume(s, c, True), 0)
+    steps(8, lambda s, c: smooth_volume(s, c, True), 0)
     pl.semaphore_wait(barrier, sum(h.astype(jnp.int32) for h in has + both))
     start(0)
     start(1)
@@ -615,7 +614,7 @@
         store_split(split_f, step, 192, apply_blocks(block_rows(), values), 2)
         return 0
 
-    lax.fori_loop(0, 12, smooth_faces, 0)
+    steps(12, smooth_faces, 0)
     inward[9].wait()
     face_field[...] += dot(give[0:192, :], split_f[0:384, :])
     gather_faces(face_field, 0, 32, 24, compact)
@@ -632,18 +631,18 @@
         split_faces(step, face_state)
         return 0
 
-    lax.fori_loop(0, 12, split_face_state, 0)
+    steps(12, split_face_state, 0)
     state_c[32:128, :] = dot(pick_face[...], split_f[0:384, :])
 
     receive(0, compact, -1.0)
     scatter_faces(compact, 32, 24, jump)
-    lax.fori_loop(0, 12, smooth_faces, 0)
+    steps(12, smooth_faces, 0)
     face_field[...] += dot(give[0:192, :], split_f[0:384, :])
     field[...] = base[...] + dot(give[192:320, :], split_f[0:384, :])
     gather_faces(face_field, 0, 32, 24, compact)
     own_part(compact, own)
     scatter_faces(own, 32, 24, jump)
-    lax.fori_loop(0, 8, split_field, 0)
+    steps(8, split_field, 0)
     cot[...] = dot(volume[...], split_n[...])
 
     def residual_volume(step, _):
@@ -652,7 +651,7 @@
         store_split(split_n, step, 128, resid, 3)
         return 0
 
-    lax.fori_loop(0, 8, residual_volume, 0)
+    steps(8, residual_volume, 0)
     field_c[...] = dot(restrict[...], split_n[...])
 
     def write_state(f, first, slot, value):
@@ -672,18 +671,18 @@
         store_split(split_l, step, 96, load(line_field, rows_of(step)), 2)
         return 0
 
-    lax.fori_loop(0, 6, split_lines, 0)
+    steps(6, split_lines, 0)
     across[...] = dot(lines[...], split_l[...])
-    receive(2, compact, 1.0)
-    scatter_faces(compact, 32, 24, near)
-    neighbour(32, FINE_FACE, start_face, 0, near_state, across, signs, near, jump)
+    neighbour(32, FINE_FACE, start_face, 0, near_state, across, signs, jump)
+    receive(2, compact, -1.0)
+    scatter_faces(compact, 32, 24, jump, True)
 
     def residual_faces(step, _):
         values = face_pull(step, load(jump, rows_of(step)), face_state, 0, 2)
         store_split(split_f, step, 192, values, 3)
         return 0
 
-    lax.fori_loop(0, 12, residual_faces, 0)
+    steps(12, residual_faces, 0)
     field_c[...] += dot(restrict_give[...], split_f[...])
 
     def coarse_first(step, _):
@@ -691,7 +690,7 @@
         store(base_c, rows, apply_blocks(block_rows(), load(field_c, rows)))
         return 0
 
-    lax.fori_loop(0, 14, coarse_first, 0)
+    steps(14, coarse_first, 0)
     gather_faces(base_c, 32, 16, 8, compact_c)
     pack(3, lambda f, first, slot: compact_c[f, first : first + slot, :], 48)
     start(3)
@@ -704,7 +703,7 @@
         store_split(split_c, step, 32, load(base_c, rows_of(step)), 2)
         return 0
 
-    lax.fori_loop(0, 2, split_coarse, 0)
+    steps(2, split_coarse, 0)
     cot_c[...] = dot(volume_c[0:96, :], split_c[0:64, :])
 
     def coarse_volume(step, _):
@@ -717,7 +716,7 @@
         store_split(split_c, step, 32, values, 2)
         return 0
 
-    lax.fori_loop(0, 2, coarse_volume, 0)
+    steps(2, coarse_volume, 0)
     face_c[...] = dot(volume_c[96:192, :], split_c[0:64, :])
 
     def coarse_faces(step, _):
@@ -725,7 +724,7 @@
         store_split(split_cf, step, 96, apply_blocks(block_rows(), values), 2)
         return 0
 
-    lax.fori_loop(0, 6, coarse_faces, 0)
+    steps(6, coarse_faces, 0)
     face_c[...] += dot(give_c[0:96, :], split_cf[0:192, :])
     gather_faces(face_c, 0, 16, 8, compact_c)
     pack(4, lambda f, first, slot: compact_c[f, first : first + slot, :], 48)
@@ -736,12 +735,12 @@
         split_faces(step, near_state)
         return 0
 
-    lax.fori_loop(0, 12, split_near, 0)
+    steps(12, split_near, 0)
     near_state_c[...] = dot(pick_face[...], split_f[0:384, :])
 
     receive(3, compact_c, -1.0)
     scatter_faces(compact_c, 16, 8, jump_c)
-    lax.fori_loop(0, 6, coarse_faces, 0)
+    steps(6, coarse_faces, 0)
     face_c[...] += dot(give_c[0:96, :], split_cf[0:192, :])
     field_c[0:32, :] += dot(give_c[96:128, :], split_cf[0:192, :])
     gather_faces(face_c, 0, 16, 8, compact_c)
@@ -752,30 +751,28 @@
         store_split(split_c, step, 32, load(field_c, rows_of(step)), 3)
         return 0
 
-    lax.fori_loop(0, 2, split_coarse_3, 0)
+    steps(2, split_coarse_3, 0)
     field[...] += dot(extend[...], split_c[...])
-    lax.fori_loop(0, 8, split_field, 0)
+    steps(8, split_field, 0)
     cot[...] = dot(volume[...], split_n[...])
-    lax.fori_loop(0, 8, lambda s, c: smooth_volume(s, c, False), 0)
+    steps(8, lambda s, c: smooth_volume(s, c, False), 0)
     receive_lines(1, line_field)
-    lax.fori_loop(0, 6, split_lines, 0)
+    steps(6, split_lines, 0)
     across_c[...] = dot(lines_c[...], split_l[...])
-    receive(4, compact_c, 1.0)
-    scatter_faces(compact_c, 16, 8, near_c)
-    neighbour(16, COARSE_FACE, base_c, 2, near_state_c, across_c, signs_c, near_c, jump_c)
+    neighbour(16, COARSE_FACE, base_c, 2, near_state_c, across_c, signs_c, jump_c)
+    receive(4, compact_c, -1.0)
+    scatter_faces(compact_c, 16, 8, jump_c, True)
 
     def split_jump(step, _):
         store_split(split_cf, step, 96, load(jump_c, rows_of(step)), 3)
         return 0
 
-    lax.fori_loop(0, 6, split_jump, 0)
+    steps(6, split_jump, 0)
     jump[...] += dot(face_extend[...], split_cf[...])
-    lax.fori_loop(0, 12, smooth_faces, 0)
+    steps(12, smooth_faces, 0)
     base[...] += dot(give[192:320, :], split_f[0:384, :])
     for v in range(5):
-        out_r[v] = base[0:125, lanes(v)]
-    outward = pltpu.make_async_copy(out_r, out_h, out_sem)
-    outward.start()
+        out_h[v] = base[0:125, lanes(v)]
     for kind in range(5):
         for f in range(6):
             @pl.when(has[f])
@@ -786,7 +783,6 @@
             @pl.when(both[line])
             def _(level=level, line=line):
                 remote_lines[level][line].wait_send()
-    outward.wait()
 
 
 def body(*args):
@@ -799,14 +795,14 @@
         vmem((384, 640), BF16), vmem((384, 640), F32),
         vmem((192, 640), F32), vmem((192, 640), F32), vmem((192, 640), F32), vmem((192, 640), F32),
         vmem((576, 640), BF16), vmem((6, 128, 128), F32), vmem((6, 128, 128), F32),
-        vmem((192, 640), F32), vmem((192, 640), F32), vmem((384, 640), F32), vmem((96, 640), F32),
+        vmem((192, 640), F32), vmem((384, 640), F32), vmem((96, 640), F32),
         vmem((192, 640), BF16), vmem((6, 32, 128), F32), vmem((32, 128), F32), vmem((6, 16, 128), F32),
         vmem((2, 32, 128), F32), vmem((2, 16, 128), F32),
         vmem((128, 640), F32), vmem((224, 640), F32), vmem((224, 640), F32), vmem((96, 640), BF16),
         vmem((288, 640), BF16), vmem((96, 640), F32), vmem((96, 640), F32),
         vmem((6, 48, 128), F32), vmem((6, 48, 128), F32),
-        vmem((96, 640), F32), vmem((96, 640), F32), vmem((192, 640), F32), vmem((96, 640), F32),
-        vmem((25, 16, 128), F32), vmem((16, 128), F32), vmem(args[0].shape, F32),
+        vmem((96, 640), F32), vmem((192, 640), F32), vmem((96, 640), F32),
+        vmem((25, 16, 128), F32), vmem((16, 128), F32),
     ]
     fine = [vmem((rows, 128), F32) for rows in (64, 64, 16, 16, 16, 16)]
     static = [vmem((rows, 128), F32) for rows in (80, 80, 24, 24, 24, 24)]
@@ -814,7 +810,6 @@
     kinds = [*fine, *fine, *static, *static, *fine, *fine, *coarse, *coarse, *coarse, *coarse]
     sems = [
         pltpu.SemaphoreType.DMA((19,)),
-        pltpu.SemaphoreType.DMA,
         pltpu.SemaphoreType.DMA((5, 6)),
         pltpu.SemaphoreType.DMA((5, 6)),
         pltpu.SemaphoreType.DMA((2, 12)),
@@ -823,9 +818,9 @@
     anywhere = pl.BlockSpec(memory_space=pl.ANY)
     return pl.pallas_call(
         kernel,
-        out_shape=jax.ShapeDtypeStruct(args[0].shape, F32),
+        out_shape=pltpu.VMEM(args[0].shape, F32),
         in_specs=[anywhere] * (len(args) + len(constants)),
-        out_specs=anywhere,
+        out_specs=pl.BlockSpec(memory_space=pltpu.VMEM),
         scratch_shapes=raw + held + work + kinds + [vmem((2, 12, 8, 128), F32)] * 2 + sems,
         compiler_params=pltpu.CompilerParams(
             collective_id=0, has_side_effects=True, vmem_limit_bytes=60 * 1024 * 1024

time: 35.7 us -> 31.2 us (0.87)
  Pallas kernels: 33.8 us -> 30.1 us
  local copies, waits for them, and re-layouts: 1.72 us -> 0.73 us
    pallas_call x1, Pallas kernels: 33.8 us -> 30.1 us  [body(): pl.pallas_call(kernel, out_shape=pltpu.VMEM(args[0].shape, F32), in_specs...]
    unnamed x1, local copies, waits for them, and re-layouts: 1.72 us -> 0.73 us
where the time goes in v3:
time: 31.2 us; the launch traced here: 30.9 us
  Pallas kernels  30.1 us (96%)
  local copies, waits for them, and re-layouts  0.73 us (2%)
    pallas_call x1, Pallas kernels, body(): pl.pallas_call(kernel, out_shape=pltpu.VMEM(args[0].shape, F32), in_specs...  30.1 us
    unnamed x1, local copies, waits for them, and re-layouts  0.73 us

profile of v3, /device:TPU:30, one launch (start us, length us, event | category | flops | bytes accessed | tf_op | source)
XLA Modules:
  0.0 30.9 jit_solution(3552890684855609472)
XLA Ops:
  0.0 30.1 %shard_map.181 = f32[5,125,128]{2,1,0:T(8,128)S(1)} custom-call(f32[5,125,128]{2,1,0:T(8,128)} %start_h.1, f32[5,125,128]{2,1,0:T(8,128)} %source_h.1, f32[125,128]{1,0:T(8,128)} %density_h.1, f32[3,125,128]{2,1,0:T(8,128)} %velocity_h.1, f32[125,128]{1,0:T(8,128)} %pressure_h.1, f32[2,8,8]{2,1,0:T(8,128)} %shift_h.1, f32[5,5,2,8,8]{4,3,2,1,0:T(8,128)} %inverse_h.1, ...), custom_call_target="tpu_custom_call" | custom-call | tf_op jit(solution)/shard_map/pallas_call | solution.py:819
  30.1 0.7 %copy.21 = f32[5,125,128]{2,1,0:T(8,128)} copy(f32[5,125,128]{2,1,0:T(8,128)S(1)} %shard_map.181) | data formatting | bytes 640000

commit v4 on v3

--- a/solution.py
+++ b/solution.py
@@ -138,6 +138,7 @@
     face_extend = np.zeros((192, 96))
     for face in range(6):
         face_extend[32 * face : 32 * face + 32, 16 * face : 16 * face + 9] = flat
+    correct = -COARSE_FACE * give_c
     face_pick = np.zeros((96, 192))
     for face in range(6):
         for row in range(16):
@@ -153,6 +154,7 @@
         "give_c": two(-COARSE_FACE * np.concatenate([take_c @ give_c, give_c])),
         "extend": three(extend),
         "face_extend": three(face_extend),
+        "chain": three(np.concatenate([take_c @ correct, extend @ correct, volume_table(5, 128) @ extend @ correct])),
         "lines": two(line_faces(5, 32)),
         "lines_c": two(line_faces(3, 16)),
         "pick_face": two(face_pick),
@@ -242,22 +244,22 @@
 
 
 def kernel(start_h, source_h, density_h, velocity_h, pressure_h, shift_h, inverse_h, *rest):
-    tables_h, rest = rest[:12], rest[12:]
+    tables_h, rest = rest[:13], rest[13:]
     out_h, rest = rest[0], rest[1:]
     (start_r, source_r, density_r, velocity_r, pressure_r, shift_r, inverse_r), rest = rest[:7], rest[7:]
-    tables_r, rest = rest[:12], rest[12:]
+    tables_r, rest = rest[:13], rest[13:]
     (
         take, volume, give, restrict, restrict_give, volume_c, give_c, extend, face_extend,
-        lines, lines_c, pick_face,
+        chain, lines, lines_c, pick_face,
     ) = tables_r
     (
         field, source, state, base, split_n, cot,
         face_state, start_face, face_field, jump, split_f, compact, own,
         near_state, across, line_field, split_l, near_blocks, block_row, edges, signs, signs_c,
         state_c, field_c, base_c, split_c, split_cf, cot_c, jump_c, compact_c, own_c,
-        near_state_c, across_c, face_c,
+        near_state_c, near_c, across_c, face_c,
         blocks, shift,
-    ), rest = rest[:36], rest[36:]
+    ), rest = rest[:37], rest[37:]
     kinds = []
     for _ in range(5):
         kinds.append((rest[:6], rest[6:12]))
@@ -299,10 +301,10 @@
         (start_h, start_r), (tables_h[0], take), (velocity_h, velocity_r), (density_h, density_r),
         (pressure_h, pressure_r), (tables_h[1], volume), (source_h, source_r), (shift_h, shift_r),
         (inverse_h, inverse_r), (tables_h[2], give),
-    ] + [(tables_h[n], tables_r[n]) for n in range(3, 12)]
+    ] + [(tables_h[n], tables_r[n]) for n in range(3, 13)]
     inward = [pltpu.make_async_copy(a, b, in_sems.at[n]) for n, (a, b) in enumerate(order)]
-    for copy in inward:
-        copy.start()
+    for n in (0, 1, 2, 3, 4, 8, 7, 5, 6, *range(9, len(inward))):
+        inward[n].start()
 
     def lane_place(rows, dim):
         lane = lax.broadcasted_iota(jnp.int32, (rows, 128), 1)
@@ -326,9 +328,9 @@
 
         steps(6, one, 0)
 
-    def scatter_faces(source_ref, rows, whole, target, add=False):
+    def scatter_faces(source_ref, rows, whole, target, add=None):
         def put(here, v, value):
-            target[here, lanes(v)] = target[here, lanes(v)] + value if add else value
+            target[here, lanes(v)] = value if add is None else add[here, lanes(v)] + value
 
         def one(f, _):
             top = f * rows
@@ -470,7 +472,7 @@
         d, side = divmod(step // per_face, 2)
         return pull_face(values, load(state_ref, rows_of(step + offset)), d, 2 * side - 1)
 
-    def neighbour(rows, face, mine, offset, near_s, across_ref, sign_ref, target):
+    def neighbour(rows, face, mine, offset, near_s, across_ref, sign_ref, target, add):
         per_face = rows // 16
         for d in range(3):
             p, q = [n for n in range(3) if n != d]
@@ -497,8 +499,10 @@
                     pulled = [pulled[v] + top[n] * jumps[n][v] for v in range(5)]
                 inverse = [near_blocks[f, n : n + 1, :] for n in range(25)]
                 change = apply_blocks(inverse, pulled)
-                jumps_now = load(target, here)
-                store(target, here, [jumps_now[v] + face * change[v] for v in range(5)])
+                change = [face * value for value in change]
+                if add:
+                    change = [old + value for old, value in zip(load(target, here), change)]
+                store(target, here, change)
                 return 0
 
             steps(2 * per_face, one, 0)
@@ -579,6 +583,11 @@
     block_slots, block_tops = (16, 8, 8), (64, 16, 16)
     pack(1, lambda f, first, slot: block_row[first : first + slot, :], 32, block_tops, block_slots)
 
+    pl.semaphore_wait(barrier, sum(h.astype(jnp.int32) for h in has + both))
+    start(0)
+    start(1)
+    start_lines(0)
+
     inward[5].wait()
     inward[6].wait()
     for v in range(5):
@@ -603,10 +612,6 @@
 
     cot[...] = dot(volume[...], split_n[...])
     steps(8, lambda s, c: smooth_volume(s, c, True), 0)
-    pl.semaphore_wait(barrier, sum(h.astype(jnp.int32) for h in has + both))
-    start(0)
-    start(1)
-    start_lines(0)
     face_field[...] = dot(take[0:192, :], split_n[0:256, :])
 
     def smooth_faces(step, _):
@@ -621,7 +626,7 @@
     pack(2, lambda f, first, slot: compact[f, first : first + slot, :], 128)
     start(2)
     base[...] += dot(give[192:320, :], split_f[0:384, :])
-    for n in range(10, 19):
+    for n in range(10, 20):
         inward[n].wait()
 
     def split_faces(step, ref):
@@ -673,9 +678,9 @@
 
     steps(6, split_lines, 0)
     across[...] = dot(lines[...], split_l[...])
-    neighbour(32, FINE_FACE, start_face, 0, near_state, across, signs, jump)
+    neighbour(32, FINE_FACE, start_face, 0, near_state, across, signs, jump, True)
     receive(2, compact, -1.0)
-    scatter_faces(compact, 32, 24, jump, True)
+    scatter_faces(compact, 32, 24, jump, jump)
 
     def residual_faces(step, _):
         values = face_pull(step, load(jump, rows_of(step)), face_state, 0, 2)
@@ -738,15 +743,6 @@
     steps(12, split_near, 0)
     near_state_c[...] = dot(pick_face[...], split_f[0:384, :])
 
-    receive(3, compact_c, -1.0)
-    scatter_faces(compact_c, 16, 8, jump_c)
-    steps(6, coarse_faces, 0)
-    face_c[...] += dot(give_c[0:96, :], split_cf[0:192, :])
-    field_c[0:32, :] += dot(give_c[96:128, :], split_cf[0:192, :])
-    gather_faces(face_c, 0, 16, 8, compact_c)
-    own_part(compact_c, own_c)
-    scatter_faces(own_c, 16, 8, jump_c)
-
     def split_coarse_3(step, _):
         store_split(split_c, step, 32, load(field_c, rows_of(step)), 3)
         return 0
@@ -755,13 +751,28 @@
     field[...] += dot(extend[...], split_c[...])
     steps(8, split_field, 0)
     cot[...] = dot(volume[...], split_n[...])
-    steps(8, lambda s, c: smooth_volume(s, c, False), 0)
     receive_lines(1, line_field)
     steps(6, split_lines, 0)
     across_c[...] = dot(lines_c[...], split_l[...])
-    neighbour(16, COARSE_FACE, base_c, 2, near_state_c, across_c, signs_c, jump_c)
+    neighbour(16, COARSE_FACE, base_c, 2, near_state_c, across_c, signs_c, near_c, False)
+
+    def coarse_rest(step, _):
+        values = face_pull(step, load(jump_c, rows_of(step)), state_c, 2, 1)
+        store_split(split_cf, step, 96, apply_blocks(block_rows(), values), 3)
+        return 0
+
+    receive(3, compact_c, -1.0)
+    scatter_faces(compact_c, 16, 8, jump_c)
+    steps(6, coarse_rest, 0)
+    face_c[...] += dot(chain[0:96, :], split_cf[...])
+    gather_faces(face_c, 0, 16, 8, compact_c)
+    own_part(compact_c, own_c)
+    scatter_faces(own_c, 16, 8, jump_c, near_c)
+    field[...] += dot(chain[96:224, :], split_cf[...])
+    cot[...] += dot(chain[224:608, :], split_cf[...])
+    steps(8, lambda s, c: smooth_volume(s, c, False), 0)
     receive(4, compact_c, -1.0)
-    scatter_faces(compact_c, 16, 8, jump_c, True)
+    scatter_faces(compact_c, 16, 8, jump_c, jump_c)
 
     def split_jump(step, _):
         store_split(split_cf, step, 96, load(jump_c, rows_of(step)), 3)
@@ -801,7 +812,7 @@
         vmem((128, 640), F32), vmem((224, 640), F32), vmem((224, 640), F32), vmem((96, 640), BF16),
         vmem((288, 640), BF16), vmem((96, 640), F32), vmem((96, 640), F32),
         vmem((6, 48, 128), F32), vmem((6, 48, 128), F32),
-        vmem((96, 640), F32), vmem((192, 640), F32), vmem((96, 640), F32),
+        vmem((96, 640), F32), vmem((96, 640), F32), vmem((192, 640), F32), vmem((96, 640), F32),
         vmem((25, 16, 128), F32), vmem((16, 128), F32),
     ]
     fine = [vmem((rows, 128), F32) for rows in (64, 64, 16, 16, 16, 16)]
@@ -809,7 +820,7 @@
     coarse = [vmem((rows, 128), F32) for rows in (24, 24, 8, 8, 8, 8)]
     kinds = [*fine, *fine, *static, *static, *fine, *fine, *coarse, *coarse, *coarse, *coarse]
     sems = [
-        pltpu.SemaphoreType.DMA((19,)),
+        pltpu.SemaphoreType.DMA((20,)),
         pltpu.SemaphoreType.DMA((5, 6)),
         pltpu.SemaphoreType.DMA((5, 6)),
         pltpu.SemaphoreType.DMA((2, 12)),

time: 31.2 us -> 31.5 us (level)
  the two profiles are of different devices: /device:TPU:30 before, /device:TPU:13 now
where the time goes in v4:
time: 31.5 us; the launch traced here: 31.4 us
  Pallas kernels  30.7 us (97%)
  local copies, waits for them, and re-layouts  0.73 us (2%)
    pallas_call x1, Pallas kernels, body(): pl.pallas_call(kernel, out_shape=pltpu.VMEM(args[0].shape, F32), in_specs...  30.7 us
    unnamed x1, local copies, waits for them, and re-layouts  0.73 us

profile of v4, /device:TPU:13, one launch (start us, length us, event | category | flops | bytes accessed | tf_op | source)
XLA Modules:
  0.0 31.4 jit_solution(6175347208180035642)
XLA Ops:
  0.0 30.7 %shard_map.190 = f32[5,125,128]{2,1,0:T(8,128)S(1)} custom-call(f32[5,125,128]{2,1,0:T(8,128)} %start_h.1, f32[5,125,128]{2,1,0:T(8,128)} %source_h.1, f32[125,128]{1,0:T(8,128)} %density_h.1, f32[3,125,128]{2,1,0:T(8,128)} %velocity_h.1, f32[125,128]{1,0:T(8,128)} %pressure_h.1, f32[2,8,8]{2,1,0:T(8,128)} %shift_h.1, f32[5,5,2,8,8]{4,3,2,1,0:T(8,128)} %inverse_h.1, ...), custom_call_target="tpu_custom_call" | custom-call | tf_op jit(solution)/shard_map/pallas_call | solution.py:830
  30.7 0.7 %copy.22 = f32[5,125,128]{2,1,0:T(8,128)} copy(f32[5,125,128]{2,1,0:T(8,128)S(1)} %shard_map.190) | data formatting | bytes 640000

commit v5 on v4

--- a/solution.py
+++ b/solution.py
@@ -328,7 +328,7 @@
 
         steps(6, one, 0)
 
-    def scatter_faces(source_ref, rows, whole, target, add=None):
+    def scatter_faces(source_ref, rows, whole, target, add=None, faces=range(6)):
         def put(here, v, value):
             target[here, lanes(v)] = value if add is None else add[here, lanes(v)] + value
 
@@ -340,7 +340,8 @@
                 put(slice(top + whole, top + whole + 8), v, jnp.broadcast_to(last, (8, 128)))
             return 0
 
-        steps(6, one, 0)
+        for f in faces:
+            one(f, 0)
 
     def turn(value, amount):
         amount %= 128
@@ -376,8 +377,8 @@
     remote = [copies(kind) for kind in range(5)]
     remote_lines = [line_copies(level) for level in range(2)]
 
-    def pack(kind, read, height, top=0, slots=None):
-        for f in range(6):
+    def pack(kind, read, height, top=0, slots=None, faces=range(6)):
+        for f in faces:
             dim, side = divmod(f, 2)
             count, stride = COUNTS[dim], STRIDES[dim]
             target = kinds[kind][0][f]
@@ -400,8 +401,8 @@
                 packed = block if packed is None else jnp.where(where == v, block, packed)
             send_lines[level, line] = packed
 
-    def start(kind):
-        for f in range(6):
+    def start(kind, faces=range(6)):
+        for f in faces:
             @pl.when(has[f])
             def _(f=f):
                 remote[kind][f].start()
@@ -472,9 +473,9 @@
         d, side = divmod(step // per_face, 2)
         return pull_face(values, load(state_ref, rows_of(step + offset)), d, 2 * side - 1)
 
-    def neighbour(rows, face, mine, offset, near_s, across_ref, sign_ref, target, add):
+    def neighbour(rows, face, mine, offset, near_s, across_ref, sign_ref, target, add, dims):
         per_face = rows // 16
-        for d in range(3):
+        for d in dims:
             p, q = [n for n in range(3) if n != d]
 
             def one(step, _, d=d, p=p, q=q):
@@ -585,7 +586,7 @@
 
     pl.semaphore_wait(barrier, sum(h.astype(jnp.int32) for h in has + both))
     start(0)
-    start(1)
+    start(1, (2, 3, 4, 5))
     start_lines(0)
 
     inward[5].wait()
@@ -623,8 +624,8 @@
     inward[9].wait()
     face_field[...] += dot(give[0:192, :], split_f[0:384, :])
     gather_faces(face_field, 0, 32, 24, compact)
-    pack(2, lambda f, first, slot: compact[f, first : first + slot, :], 128)
-    start(2)
+    pack(2, lambda f, first, slot: compact[f, first : first + slot, :], 128, faces=(2, 3, 4, 5))
+    start(2, (2, 3, 4, 5))
     base[...] += dot(give[192:320, :], split_f[0:384, :])
     for n in range(10, 20):
         inward[n].wait()
@@ -643,8 +644,11 @@
     scatter_faces(compact, 32, 24, jump)
     steps(12, smooth_faces, 0)
     face_field[...] += dot(give[0:192, :], split_f[0:384, :])
+    gather_faces(face_field, 0, 32, 24, compact)
+    pack(2, lambda f, first, slot: compact[f, first : first + slot, :], 128, faces=(0, 1))
+    start(2, (0, 1))
+    start(1, (0, 1))
     field[...] = base[...] + dot(give[192:320, :], split_f[0:384, :])
-    gather_faces(face_field, 0, 32, 24, compact)
     own_part(compact, own)
     scatter_faces(own, 32, 24, jump)
     steps(8, split_field, 0)
@@ -665,11 +669,14 @@
     def write_blocks(f, first, slot, value):
         near_blocks[f, first : first + slot, :] = value
 
-    for f in range(6):
-        arrive(1, f)
-        unpack(1, f, 128, write_state, 1.0, tops, slots)
-        unpack(1, f, 32, write_blocks, 1.0, block_tops, block_slots)
-    scatter_faces(compact, 32, 24, near_state)
+    def receive_state(faces):
+        for f in faces:
+            arrive(1, f)
+            unpack(1, f, 128, write_state, 1.0, tops, slots)
+            unpack(1, f, 32, write_blocks, 1.0, block_tops, block_slots)
+        scatter_faces(compact, 32, 24, near_state, faces=faces)
+
+    receive_state((2, 3, 4, 5))
     receive_lines(0, line_field)
 
     def split_lines(step, _):
@@ -678,7 +685,7 @@
 
     steps(6, split_lines, 0)
     across[...] = dot(lines[...], split_l[...])
-    neighbour(32, FINE_FACE, start_face, 0, near_state, across, signs, jump, True)
+    neighbour(32, FINE_FACE, start_face, 0, near_state, across, signs, jump, True, (1, 2))
     receive(2, compact, -1.0)
     scatter_faces(compact, 32, 24, jump, jump)
 
@@ -736,6 +743,8 @@
     start(4)
     field_c[0:32, :] += dot(give_c[96:128, :], split_cf[0:192, :])
 
+    receive_state((0, 1))
+
     def split_near(step, _):
         split_faces(step, near_state)
         return 0
@@ -754,7 +763,7 @@
     receive_lines(1, line_field)
     steps(6, split_lines, 0)
     across_c[...] = dot(lines_c[...], split_l[...])
-    neighbour(16, COARSE_FACE, base_c, 2, near_state_c, across_c, signs_c, near_c, False)
+    neighbour(16, COARSE_FACE, base_c, 2, near_state_c, across_c, signs_c, near_c, False, (0, 1, 2))
 
     def coarse_rest(step, _):
         values = face_pull(step, load(jump_c, rows_of(step)), state_c, 2, 1)

time: 31.5 us -> 32.5 us (1.032)
  Pallas kernels: 30.7 us -> 31.7 us
    pallas_call x1, Pallas kernels: 30.7 us -> 31.7 us  [body(): pl.pallas_call(kernel, out_shape=pltpu.VMEM(args[0].shape, F32), in_specs...]
where the time goes in v5:
time: 32.5 us
  Pallas kernels  31.7 us (98%)
  local copies, waits for them, and re-layouts  0.73 us (2%)
    pallas_call x1, Pallas kernels, body(): pl.pallas_call(kernel, out_shape=pltpu.VMEM(args[0].shape, F32), in_specs...  31.7 us
    unnamed x1, local copies, waits for them, and re-layouts  0.73 us

profile of v5, /device:TPU:13, one launch (start us, length us, event | category | flops | bytes accessed | tf_op | source)
XLA Modules:
  0.0 32.5 jit_solution(5015747572764926242)
XLA Ops:
  0.0 31.7 %shard_map.190 = f32[5,125,128]{2,1,0:T(8,128)S(1)} custom-call(f32[5,125,128]{2,1,0:T(8,128)} %start_h.1, f32[5,125,128]{2,1,0:T(8,128)} %source_h.1, f32[125,128]{1,0:T(8,128)} %density_h.1, f32[3,125,128]{2,1,0:T(8,128)} %velocity_h.1, f32[125,128]{1,0:T(8,128)} %pressure_h.1, f32[2,8,8]{2,1,0:T(8,128)} %shift_h.1, f32[5,5,2,8,8]{4,3,2,1,0:T(8,128)} %inverse_h.1, ...), custom_call_target="tpu_custom_call" | custom-call | tf_op jit(solution)/shard_map/pallas_call | solution.py:839
  31.7 0.7 %copy.22 = f32[5,125,128]{2,1,0:T(8,128)} copy(f32[5,125,128]{2,1,0:T(8,128)S(1)} %shard_map.190) | data formatting | bytes 640000

commit v6 on v4

--- a/solution.py
+++ b/solution.py
@@ -401,7 +401,7 @@
             send_lines[level, line] = packed
 
     def start(kind):
-        for f in range(6):
+        for f in (2, 3, 4, 5, 0, 1):
             @pl.when(has[f])
             def _(f=f):
                 remote[kind][f].start()
@@ -583,10 +583,6 @@
     block_slots, block_tops = (16, 8, 8), (64, 16, 16)
     pack(1, lambda f, first, slot: block_row[first : first + slot, :], 32, block_tops, block_slots)
 
-    pl.semaphore_wait(barrier, sum(h.astype(jnp.int32) for h in has + both))
-    start(0)
-    start(1)
-    start_lines(0)
 
     inward[5].wait()
     inward[6].wait()
@@ -612,6 +608,10 @@
 
     cot[...] = dot(volume[...], split_n[...])
     steps(8, lambda s, c: smooth_volume(s, c, True), 0)
+    pl.semaphore_wait(barrier, sum(h.astype(jnp.int32) for h in has + both))
+    start(0)
+    start(1)
+    start_lines(0)
     face_field[...] = dot(take[0:192, :], split_n[0:256, :])
 
     def smooth_faces(step, _):

time: 31.5 us -> 31.5 us (level)
  the two profiles are of different devices: /device:TPU:13 before, /device:TPU:11 now
where the time goes in v6:
time: 31.5 us; the launch traced here: 31.4 us
  Pallas kernels  30.7 us (97%)
  local copies, waits for them, and re-layouts  0.73 us (2%)
    pallas_call x1, Pallas kernels, body(): pl.pallas_call(kernel, out_shape=pltpu.VMEM(args[0].shape, F32), in_specs...  30.7 us
    unnamed x1, local copies, waits for them, and re-layouts  0.73 us

profile of v6, /device:TPU:11, one launch (start us, length us, event | category | flops | bytes accessed | tf_op | source)
XLA Modules:
  0.0 31.4 jit_solution(2075688156506043913)
XLA Ops:
  0.0 30.7 %shard_map.190 = f32[5,125,128]{2,1,0:T(8,128)S(1)} custom-call(f32[5,125,128]{2,1,0:T(8,128)} %start_h.1, f32[5,125,128]{2,1,0:T(8,128)} %source_h.1, f32[125,128]{1,0:T(8,128)} %density_h.1, f32[3,125,128]{2,1,0:T(8,128)} %velocity_h.1, f32[125,128]{1,0:T(8,128)} %pressure_h.1, f32[2,8,8]{2,1,0:T(8,128)} %shift_h.1, f32[5,5,2,8,8]{4,3,2,1,0:T(8,128)} %inverse_h.1, ...), custom_call_target="tpu_custom_call" | custom-call | tf_op jit(solution)/shard_map/pallas_call | solution.py:830
  30.7 0.7 %copy.22 = f32[5,125,128]{2,1,0:T(8,128)} copy(f32[5,125,128]{2,1,0:T(8,128)S(1)} %shard_map.190) | data formatting | bytes 640000

commit v7 on v5

--- a/solution.py
+++ b/solution.py
@@ -401,7 +401,7 @@
                 packed = block if packed is None else jnp.where(where == v, block, packed)
             send_lines[level, line] = packed
 
-    def start(kind, faces=range(6)):
+    def start(kind, faces=(2, 3, 4, 5, 0, 1)):
         for f in faces:
             @pl.when(has[f])
             def _(f=f):
@@ -584,10 +584,6 @@
     block_slots, block_tops = (16, 8, 8), (64, 16, 16)
     pack(1, lambda f, first, slot: block_row[first : first + slot, :], 32, block_tops, block_slots)
 
-    pl.semaphore_wait(barrier, sum(h.astype(jnp.int32) for h in has + both))
-    start(0)
-    start(1, (2, 3, 4, 5))
-    start_lines(0)
 
     inward[5].wait()
     inward[6].wait()
@@ -613,6 +609,10 @@
 
     cot[...] = dot(volume[...], split_n[...])
     steps(8, lambda s, c: smooth_volume(s, c, True), 0)
+    pl.semaphore_wait(barrier, sum(h.astype(jnp.int32) for h in has + both))
+    start(0)
+    start(1, (2, 3, 4, 5))
+    start_lines(0)
     face_field[...] = dot(take[0:192, :], split_n[0:256, :])
 
     def smooth_faces(step, _):

time: 32.5 us -> 30.9 us (0.951)
  the two profiles are of different devices: /device:TPU:13 before, /device:TPU:23 now
where the time goes in v7:
time: 30.9 us
  Pallas kernels  30.1 us (97%)
  local copies, waits for them, and re-layouts  0.73 us (2%)
    pallas_call x1, Pallas kernels, body(): pl.pallas_call(kernel, out_shape=pltpu.VMEM(args[0].shape, F32), in_specs...  30.1 us
    unnamed x1, local copies, waits for them, and re-layouts  0.73 us

profile of v7, /device:TPU:23, one launch (start us, length us, event | category | flops | bytes accessed | tf_op | source)
XLA Modules:
  0.0 30.9 jit_solution(7524987702655470506)
XLA Ops:
  0.0 30.1 %shard_map.190 = f32[5,125,128]{2,1,0:T(8,128)S(1)} custom-call(f32[5,125,128]{2,1,0:T(8,128)} %start_h.1, f32[5,125,128]{2,1,0:T(8,128)} %source_h.1, f32[125,128]{1,0:T(8,128)} %density_h.1, f32[3,125,128]{2,1,0:T(8,128)} %velocity_h.1, f32[125,128]{1,0:T(8,128)} %pressure_h.1, f32[2,8,8]{2,1,0:T(8,128)} %shift_h.1, f32[5,5,2,8,8]{4,3,2,1,0:T(8,128)} %inverse_h.1, ...), custom_call_target="tpu_custom_call" | custom-call | tf_op jit(solution)/shard_map/pallas_call | solution.py:839
  30.1 0.7 %copy.22 = f32[5,125,128]{2,1,0:T(8,128)} copy(f32[5,125,128]{2,1,0:T(8,128)S(1)} %shard_map.190) | data formatting | bytes 640000
